TPU v7x, 128 devices: a whole 4x4x4 slice. The times are simulated.
128 devices in a mesh: row: 8 (over x, core), col: 16 (over z, y).
Axes of the slice: x: 4, y: 4, z: 4, core: 2. Of those that a mesh axis runs over, the one named last changes fastest.
Arguments:
- kernel: float32 [16, 8, 128, 8, 16, 128], P(None, 'row', None, None, 'col'), as said below
Outputs:
- factored: float32 [16, 8, 128, 8, 16, 128], P(None, 'row', None, None, 'col')
Inputs may be any that keep to these rules, and one draw needn't show every extreme that they name: kernel is symmetric and positive definite, with a diagonal that dominates in norm.
All inputs are finite; a program needn't handle non-finite values.
Results may differ from a plain program's by a relative error of at most 0.0001.
Values sent between devices are 32-bit elements; how exact they have to be, the bound alone decides.
No kernel may reach another device: no remote copies, remote signals or barrier semaphores. Data moves between devices by JAX's collectives and lax.ppermute only.
A program may use at most 128 MiB of HBM per device.

v0:
```python
import jax
import jax.numpy as jnp
from jax import lax
from jax.sharding import PartitionSpec as P


def spread(value, axis, source):
    kept = jnp.where(lax.axis_index(axis) == source, value, 0).astype(value.dtype)
    return lax.psum(kept, axis)


def factor_group(matrix, first_block, group_size):
    row_count = lax.axis_size("row")
    col_count = lax.axis_size("col")
    row_here = lax.axis_index("row")
    col_here = lax.axis_index("col")
    blocks_r, block_size, blocks_c, _ = matrix.shape
    row_blocks = jnp.arange(blocks_r, dtype=jnp.int32) * row_count + row_here
    col_blocks = jnp.arange(blocks_c, dtype=jnp.int32) * col_count + col_here
    b = 0
    k = first_block + b
    pieces = spread(matrix[:, :, k // col_count, :], "col", k % col_count)
    b = 0
    k = first_block + b
    strips = spread(pieces[k // row_count], "row", k % row_count)
    factor = jnp.linalg.cholesky(strips)
    identity = jnp.eye(group_size * block_size, dtype=strips.dtype)
    inverse = lax.linalg.triangular_solve(factor, identity, left_side=True, lower=True)
    under_rows = jnp.einsum("inw,vw->inv", pieces, inverse, precision=lax.Precision.HIGHEST)
    picked = jnp.take(
        factor.reshape(group_size, block_size, group_size * block_size),
        jnp.clip(row_blocks - first_block, 0, group_size - 1),
        axis=0,
    )
    tail_rows = (row_blocks >= first_block + group_size)[:, None, None]
    in_group = (row_blocks >= first_block)[:, None, None]
    row_terms = jnp.where(tail_rows, under_rows, 0.0)
    factored = jnp.where(tail_rows, under_rows, jnp.where(in_group, picked, 0.0))
    per_owner = col_count // row_count
    gathered = lax.all_gather(factored[None], "row", axis=0, tiled=True)
    chosen = lax.dynamic_index_in_dim(gathered, col_here % row_count, 0, keepdims=False)
    col_terms = lax.dynamic_index_in_dim(
        chosen.reshape(blocks_c, per_owner, block_size, group_size * block_size),
        col_here // row_count,
        1,
        keepdims=False,
    )
    col_terms = jnp.where((col_blocks >= first_block + group_size)[:, None, None], col_terms, 0.0)
    update = jnp.einsum("inw,jmw->injm", row_terms, col_terms, precision=lax.Precision.HIGHEST)
    result = matrix - update
    b = 0
    k = first_block + b
    local_col = k // col_count
    current = result[:, :, local_col, :]
    result = result.at[:, :, local_col, :].set(
        jnp.where(col_here == k % col_count, factored, current)
    )
    upper_part = ((row_blocks >= first_block) & (row_blocks < first_block + group_size))[
        :, None, None, None
    ] & (col_blocks >= first_block + group_size)[None, None, :, None]
    return jnp.where(upper_part, 0.0, result)


def local(kernel):
    blocks_r, _, block_size, blocks_c, _, _ = kernel.shape
    matrix = kernel.reshape(blocks_r, block_size, blocks_c, block_size)
    matrix = factor_group(matrix, 0, 1)
    matrix = factor_group(matrix, 1, 1)
    return matrix.reshape(kernel.shape)


def solution(mesh):
    placed = (P(None, "row", None, None, "col", None),)
    return jax.shard_map(
        local,
        mesh=mesh,
        in_specs=placed,
        out_specs=P(None, "row", None, None, "col", None),
        check_vma=False,
    )
```

profile of v0, /device:TPU:15, one launch (start us, length us, event | category | flops | bytes accessed | tf_op | source)
XLA Modules:
  0.0 539.8 jit_solution(16497278113813406978)
XLA Ops:
  6.5 20.5 %copy.36 = f32[16,1,128,8,1,128]{2,5,0,3,4,1:T(8,128)} copy(f32[16,1,128,8,1,128]{5,4,3,2,1,0:T(1,128)} %param.10) | data formatting | bytes 16777216 | tf_op args[0]
  27.0 2.3 fusion.7
  29.5 87.6 %all-reduce.5.cloned.1.call-done = f32[16,128,128]{1,2,0:T(8,128)} async-done(((f32[16,128,128]{1,2,0:T(8,128)}), f32[16,128,128]{1,2,0:T(8,128)}) %all-reduce.5.cloned.1.call-update) | async-done | bytes 1048592 | tf_op jit(solution)/shard_map/psum | solution.py:9
  117.0 1.5 fusion.29
  118.6 58.9 %all-reduce.7.cloned.1.call-done = f32[128,128]{0,1:T(8,128)} async-done(((f32[128,128]{0,1:T(8,128)}), f32[128,128]{0,1:T(8,128)}) %all-reduce.7.cloned.1.call-update) | async-done | bytes 65552 | tf_op jit(solution)/shard_map/psum | solution.py:9
  179.3 11.7 %cholesky.44 = f32[128,128]{1,0:T(8,128)S(1)} custom-call(f32[128,128]{1,0:T(8,128)S(1)} %fusion.33), custom_call_target="Cholesky" | custom-call | tf_op jit(solution)/shard_map/jit(cholesky)/cholesky | solution.py:26
  192.5 9.8 %custom-call.6 = f32[1,128,128]{1,2,0:T(8,128)S(1)} custom-call(f32[1,128,128]{2,1,0:T(8,128)S(1)} %get-tuple-element.34), custom_call_target="InvertDiagBlocksLowerTriangular" | custom-call | tf_op jit(solution)/shard_map/triangular_solve/custom-call.0 | solution.py:28
  202.6 2.4 fusion.11
  205.0 1.4 copy.42
  206.8 48.7 %all-gather.5.cloned.1.call-done = f32[128,128,128]{2,1,0:T(8,128)} async-done(((f32[16,128,128]{2,1,0:T(8,128)}), f32[128,128,128]{2,1,0:T(8,128)}) %all-gather.5.cloned.1.call-update) | async-done | bytes 8388624 | tf_op jit(solution)/shard_map/all_gather | solution.py:40
  255.4 1.3 constant_dynamic-slice_fusion.1
  256.7 9.7 %convolution_subtract_fusion.1 = f32[16,128,8,128]{1,3,0,2:T(8,128)S(1)} fusion(f32[16,128,128]{1,2,0:T(8,128)S(1)} %get-tuple-element.37, f32[8,2,128,128]{3,2,1,0:T(8,128)S(1)} %bitcast.96, s32[]{:T(128)S(6)} %select_n.134, pred[16]{0:T(512)(128)(4,1)S(1)} %get-tuple-element.45, pred[8]{0:T(512)(128)(4,1)S(1)} %fusion.37, f32[16,1,128,8,1,128]{2,5,0,3,4,1:T(8,128)} %copy.36), kind=kOutput, calls=%fused_computation.3 | convolution fusion | flops 3223715840 | bytes 18351108 | tf_op jit(solution)/shard_map/inw,jmw->injm/dot_general | solution.py:49
  267.3 3.4 copy-done
  271.9 86.8 %all-reduce.9.cloned.1.call-done = f32[16,128,128]{1,2,0:T(8,128)} async-done(((f32[16,128,128]{1,2,0:T(8,128)}), f32[16,128,128]{1,2,0:T(8,128)}) %all-reduce.9.cloned.1.call-update) | async-done | bytes 1048592 | tf_op jit(solution)/shard_map/psum | solution.py:9
  358.7 1.5 fusion.28
  360.5 58.7 %all-reduce.11.cloned.1.call-done = f32[128,128]{0,1:T(8,128)} async-done(((f32[128,128]{0,1:T(8,128)}), f32[128,128]{0,1:T(8,128)}) %all-reduce.11.cloned.1.call-update) | async-done | bytes 65552 | tf_op jit(solution)/shard_map/psum | solution.py:9
  421.0 11.7 %cholesky.55 = f32[128,128]{1,0:T(8,128)S(1)} custom-call(f32[128,128]{1,0:T(8,128)S(1)} %fusion.31), custom_call_target="Cholesky" | custom-call | tf_op jit(solution)/shard_map/jit(cholesky)/cholesky | solution.py:26
  434.2 9.8 %custom-call.7 = f32[1,128,128]{1,2,0:T(8,128)S(1)} custom-call(f32[1,128,128]{2,1,0:T(8,128)S(1)} %get-tuple-element.32), custom_call_target="InvertDiagBlocksLowerTriangular" | custom-call | tf_op jit(solution)/shard_map/triangular_solve/custom-call.0 | solution.py:28
  444.3 2.4 fusion.10
  446.6 1.4 copy.50
  448.1 48.9 %all-gather.7.cloned.1.call-done = f32[128,128,128]{2,1,0:T(8,128)} async-done(((f32[16,128,128]{2,1,0:T(8,128)}), f32[128,128,128]{2,1,0:T(8,128)}) %all-gather.7.cloned.1.call-update) | async-done | bytes 8388624 | tf_op jit(solution)/shard_map/all_gather | solution.py:40
  498.4 9.9 %convolution_subtract_fusion = f32[16,128,8,128]{1,3,0,2:T(8,128)S(1)} fusion(f32[16,128,8,128]{1,3,0,2:T(8,128)} %copy-done, f32[16,128,128]{1,2,0:T(8,128)S(1)} %get-tuple-element.39, f32[8,2,128,128]{3,2,1,0:T(8,128)S(1)} %bitcast.95, s32[]{:T(128)S(6)} %select_n.134, pred[16]{0:T(512)(128)(4,1)S(1)} %broadcast_compare_fusion.1, pred[8]{0:T(512)(128)(4,1)S(1)} %fusion.38), kind=kOutput, calls=%fused_computation.2 | convolution fusion | flops 3223715840 | bytes 18351108 | tf_op jit(solution)/shard_map/inw,jmw->injm/dot_general | solution.py:49
  508.5 3.9 select_bitcast_fusion
  512.4 20.5 %copy.53 = f32[16,1,128,8,1,128]{5,4,3,2,1,0:T(1,128)} copy(f32[16,1,128,8,1,128]{2,5,0,3,4,1:T(8,128)} %select_bitcast_fusion) | data formatting | bytes 16777216 | tf_op jit(solution)/shard_map/reshape | solution.py:69
  (40 shorter events, 11.5 us)
Async XLA Ops:
  6.5 110.5 %all-reduce.5.cloned.1.call-start = ((), (), s32[]{:S(2)}) async-start(), calls=%async_computation | async-start | bytes 2097152 | tf_op jit(solution)/shard_map/psum | solution.py:9
  29.4 148.1 %all-reduce.7.cloned.1.call-start = ((), (), s32[]{:S(2)}) async-start(), calls=%async_computation.1 | async-start | bytes 131072 | tf_op jit(solution)/shard_map/psum | solution.py:9
  118.5 136.9 %all-gather.5.cloned.1.call-start = ((), (), s32[]{:S(2)}) async-start(), calls=%async_computation.4 | async-start | bytes 9437184 | tf_op jit(solution)/shard_map/all_gather | solution.py:40
  206.4 152.3 %all-reduce.9.cloned.1.call-start = ((), (), s32[]{:S(2)}) async-start(), calls=%async_computation.2 | async-start | bytes 2097152 | tf_op jit(solution)/shard_map/psum | solution.py:9
  267.3 3.4 copy-start
  271.8 147.4 %all-reduce.11.cloned.1.call-start = ((), (), s32[]{:S(2)}) async-start(), calls=%async_computation.3 | async-start | bytes 131072 | tf_op jit(solution)/shard_map/psum | solution.py:9
  360.2 136.9 %all-gather.7.cloned.1.call-start = ((), (), s32[]{:S(2)}) async-start(), calls=%async_computation.5 | async-start | bytes 9437184 | tf_op jit(solution)/shard_map/all_gather | solution.py:40
Sparse Core Ops, SparseCore 0:
  29.5 87.4 all-reduce.4
  119.3 58.1 all-reduce.6
  206.6 48.8 all-gather.4
  271.9 86.7 all-reduce.8
  361.0 58.1 all-reduce.10
  448.2 48.8 all-gather.6
where the time goes:
time: 544 us; the launch traced here: 540 us
  waiting for transfers between devices  390 us (72%)
  other arithmetic  59.1 us (11%)
  local copies, waits for them, and re-layouts  51.8 us (10%)
  matrix products  24.9 us (5%)
  between operations  13.7 us (3%)
    psum x4, waiting for transfers between devices, spread(): return lax.psum(kept, axis)  292 us
    all_gather x2, waiting for transfers between devices, factor_group(): gathered = lax.all_gather(factored[None], 'row', axis=0, tiled=True)  97.6 us
    another operation x6, other arithmetic, factor_group(): factor = jnp.linalg.cholesky(strips)  24.9 us
    unnamed x3, local copies, waits for them, and re-layouts  23.9 us
    another operation x4, other arithmetic, factor_group(): lax.linalg.triangular_solve(factor, identity, left_side=True, lower=True)  20.9 us
    reshape x1, local copies, waits for them, and re-layouts, local(): return matrix.reshape(kernel.shape)  20.5 us
    dot_general x2, matrix products, factor_group(): jnp.einsum('inw,jmw->injm', row_terms, col_terms, precision=lax.Precision...  19.6 us
  transfers between devices with their start and end apart: 6, of which 6 were waited for; matrix products, arithmetic and copies ran while one was open for 0% of the time, Pallas kernels for 0%

commit v1 on v0

v1 whole, which is shorter than its diff:
```python
import jax
import jax.numpy as jnp
from jax import lax
from jax.experimental import pallas as pl
from jax.experimental.pallas import tpu as pltpu
from jax.sharding import PartitionSpec as P

F32 = jnp.float32
BF16 = jnp.bfloat16
BOTH = ("row", "col")
NB = 128
W2 = 2 * NB
TR = 256


def split2(x):
    high = x.astype(BF16)
    return high, (x - high.astype(F32)).astype(BF16)


def factor_kernel(where_ref, mine_ref, other_ref, lower_ref, inverse_ref, s_ref):
    core = where_ref[0]
    size, sub_rows, group = W2, 8, 32

    def place(first, second):
        s_ref[0:NB, 0:NB] = first[0]
        s_ref[NB:W2, 0:NB] = second[0]
        s_ref[0:NB, NB:W2] = second[0].T
        s_ref[NB:W2, NB:W2] = second[1]

    @pl.when(core == 0)
    def _():
        place(mine_ref, other_ref)

    @pl.when(core == 1)
    def _():
        place(other_ref, mine_ref)

    rows = lax.broadcasted_iota(jnp.int32, (size, size), 0)
    cols = lax.broadcasted_iota(jnp.int32, (size, size), 1)
    s_ref[:, size:] = jnp.where(rows == cols, 1.0, 0.0)
    sub = lax.broadcasted_iota(jnp.int32, (sub_rows, NB), 0)
    tiles = 3
    width = NB * tiles
    panels = group // sub_rows
    for o in range(0, size, group):
        lo = (o // NB) * NB
        r = [
            [
                s_ref[o + sub_rows * q : o + sub_rows * (q + 1), lo + NB * t : lo + NB * (t + 1)]
                for t in range(tiles)
            ]
            for q in range(panels)
        ]
        for p in range(panels):
            oo = o - lo + p * sub_rows
            c = [
                [jnp.broadcast_to(r[q][0][:, oo + j : oo + j + 1], (sub_rows, NB)) for j in range(sub_rows)]
                if q >= p
                else None
                for q in range(panels)
            ]
            b = [
                [
                    jnp.broadcast_to(c[p][j][i : i + 1, :], (sub_rows, NB)) if i >= j else None
                    for j in range(sub_rows)
                ]
                for i in range(sub_rows)
            ]
            scale = None
            for k in range(sub_rows):
                s = lax.rsqrt(b[k][k])
                scale = s if scale is None else jnp.where(sub >= k, s, scale)
                m = [None] * sub_rows
                for i in range(k + 1, sub_rows):
                    m[i] = b[i][k] * s
                for i in range(k + 1, sub_rows):
                    for j in range(k + 1, i + 1):
                        b[i][j] = b[i][j] - m[i] * m[j]
                u = [jnp.broadcast_to(r[p][t][k : k + 1, :], (sub_rows, NB)) * s for t in range(tiles)]
                for q in range(p, panels):
                    mult = c[q][k] * s
                    for j in range(k + 1, sub_rows):
                        c[q][j] = c[q][j] - mult * m[j]
                    if q == p:
                        if k == sub_rows - 1:
                            continue
                        mult = jnp.where(sub > k, mult, 0.0)
                    r[q] = [r[q][t] - mult * u[t] for t in range(tiles)]
            for t in range(tiles):
                s_ref[
                    o + sub_rows * p : o + sub_rows * (p + 1), lo + NB * t : lo + NB * (t + 1)
                ] = r[p][t] * scale
        if o + group < size:
            lo2 = ((o + group) // NB) * NB
            uu = s_ref[o : o + group, lo2 : lo + width]
            left = size - lo2
            h = uu.astype(BF16).astype(F32)
            rest = uu - h
            mid = rest.astype(BF16).astype(F32)
            low = rest - mid
            lhs = jnp.concatenate([h, h, mid, h, low, mid], axis=0)[:, :left].astype(BF16)
            rhs = jnp.concatenate([h, mid, h, low, h, mid], axis=0).astype(BF16)
            update = lax.dot_general(lhs, rhs, (((0,), (0,)), ((), ())), preferred_element_type=F32)
            skip = o + group - lo2
            s_ref[o + group : size, lo2 : lo + width] = (
                s_ref[o + group : size, lo2 : lo + width] - update[skip:, :]
            )
    lower_ref[...] = jnp.where(cols >= rows, s_ref[:, 0:size], 0.0).T
    inverse_ref[...] = jnp.where(cols <= rows, s_ref[:, size:], 0.0)


def factor_corner(place, mine, other):
    vmem = pl.BlockSpec(memory_space=pltpu.VMEM)
    return pl.pallas_call(
        factor_kernel,
        out_shape=(jax.ShapeDtypeStruct((W2, W2), F32),) * 2,
        in_specs=[pl.BlockSpec(memory_space=pltpu.SMEM), vmem, vmem],
        out_specs=(vmem, vmem),
        scratch_shapes=[pltpu.VMEM((W2, 2 * W2), F32)],
        compiler_params=pltpu.CompilerParams(vmem_limit_bytes=8 * 1024 * 1024),
        cost_estimate=pl.CostEstimate(flops=20_000_000, bytes_accessed=1_000_000, transcendentals=256),
        name="corner_factor",
    )(place, mine, other)


def trailing_kernel(
    place_ref, lower_ref, inverse_ref, g_ref, gp_ref, gm_ref, rp_ref, rm_ref, cmine_ref, cother_ref, m_ref,
    o_ref, a_ref, lt_ref, wc_ref, sems,
):
    step = pl.program_id(0)
    row, col, core, z, y = (place_ref[n] for n in range(5))

    @pl.when(step == 0)
    def _():
        copies = [
            pltpu.make_async_copy(src, dst, sems.at[n])
            for n, (src, dst) in enumerate(
                [
                    (g_ref, a_ref.at[0:4]),
                    (gm_ref, a_ref.at[4:8]),
                    (rp_ref, a_ref.at[8:10]),
                    (rm_ref, a_ref.at[10:12]),
                    (gp_ref, a_ref.at[12:16]),
                ]
            )
        ]
        for copy in copies:
            copy.start()
        inverse = inverse_ref[...]
        high, low = split2(inverse.T)
        lt_ref[0:W2, :] = high
        lt_ref[W2 : 2 * W2, :] = low
        lt_ref[2 * W2 : 3 * W2, :] = high
        high, low = split2(inverse)
        lhs = jnp.concatenate([high, high, low], axis=1)

        def columns(first, second):
            for j in range(0, 8, 2):
                x = jnp.concatenate(
                    [
                        jnp.concatenate([ref[:, jj, :] for ref in (first, second)], axis=0)
                        for jj in (j, j + 1)
                    ],
                    axis=1,
                )
                xh, xl = split2(x)
                w = jnp.dot(lhs, jnp.concatenate([xh, xl, xh], axis=0), preferred_element_type=F32)
                wh, wl = split2(w)
                span = pl.ds(j * NB, W2)
                wc_ref[0:W2, span] = wh
                wc_ref[W2 : 2 * W2, span] = wl
                wc_ref[2 * W2 : 3 * W2, span] = wh

        @pl.when(core == 0)
        def _():
            columns(cmine_ref, cother_ref)

        @pl.when(core == 1)
        def _():
            columns(cother_ref, cmine_ref)

        for copy in copies:
            copy.wait()

    half = step // 4
    zfirst = ((step // 2 - z + 4) % 4) * 4 + step % 2
    unit0 = jnp.where(core == 0, zfirst, ((3 * half - y + 4) % 4) * 4 + step % 4)
    unit1 = jnp.where(core == 0, zfirst + 2, ((1 + half - y + 4) % 4) * 4 + step % 4)
    a = jnp.concatenate([a_ref[unit0], a_ref[unit1]], axis=1)
    ah, al = split2(a)
    w = jnp.dot(jnp.concatenate([ah, ah, al], axis=1), lt_ref[...], preferred_element_type=F32)
    wh, wl = split2(w)
    u = jnp.dot(jnp.concatenate([wh, wh, wl], axis=1), wc_ref[...], preferred_element_type=F32)
    o_ref[...] = m_ref[...] - u.reshape(TR, 8, NB)

    @pl.when(col == 0)
    def _():
        o_ref[:, 0, :] = w[:, 0:NB]

    @pl.when(col == 1)
    def _():
        o_ref[:, 0, :] = w[:, NB:W2]

    @pl.when((step == 0) & (row < 2))
    def _():
        o_ref[0:NB, :, :] = jnp.zeros((NB, 8, NB), F32)

        @pl.when(col < 2)
        def _():
            o_ref[0:NB, 0, :] = lower_ref[
                pl.ds(pl.multiple_of(row * NB, NB), NB), pl.ds(pl.multiple_of(col * NB, NB), NB)
            ]


def update_trailing(place, lower, inverse, g, gp, gm, rp, rm, cmine, cother, m):
    anywhere = pl.BlockSpec(memory_space=pl.ANY)
    whole = lambda shape: pl.BlockSpec(shape, lambda i: (0,) * len(shape))
    rows = m.shape[0]
    block = pl.BlockSpec((TR, 8, NB), lambda i: (i, 0, 0))
    return pl.pallas_call(
        trailing_kernel,
        grid=(rows // TR,),
        out_shape=jax.ShapeDtypeStruct(m.shape, F32),
        in_specs=[
            pl.BlockSpec(memory_space=pltpu.SMEM),
            whole((W2, W2)),
            whole((W2, W2)),
            anywhere,
            anywhere,
            anywhere,
            anywhere,
            anywhere,
            whole((NB, 8, NB)),
            whole((NB, 8, NB)),
            block,
        ],
        out_specs=block,
        scratch_shapes=[
            pltpu.VMEM((16, TR, NB), F32),
            pltpu.VMEM((3 * W2, W2), BF16),
            pltpu.VMEM((3 * W2, 8 * NB), BF16),
            pltpu.SemaphoreType.DMA((5,)),
        ],
        compiler_params=pltpu.CompilerParams(vmem_limit_bytes=32 * 1024 * 1024),
        cost_estimate=pl.CostEstimate(flops=4_000_000_000, bytes_accessed=20_000_000, transcendentals=0),
        name="trailing_update",
    )(place, lower, inverse, g, gp, gm, rp, rm, cmine, cother, m)


def device(x, core, z, y):
    return (x % 4 * 2 + core) * 16 + z % 4 * 4 + y % 4


def pairs(moves):
    return [(device(*a), device(*b)) for a, b in moves]


SPAN = range(4)
CORES = range(2)


def along_x(hops):
    return pairs(
        [((a, k, z, y), (b, k, z, y)) for a, b in hops for k in CORES for z in SPAN for y in SPAN]
    )


def along_z(hops, cores=CORES, ys=SPAN):
    return [((x, k, a, y), (x, k, b, y)) for a, b in hops for x in SPAN for k in cores for y in ys]


def along_y(hops, cores=CORES, zs=SPAN):
    return [((x, k, z, a), (x, k, z, b)) for a, b in hops for x in SPAN for k in cores for z in zs]


SWAP = pairs([((x, k, z, y), (x, 1 - k, z, y)) for x in SPAN for k in CORES for z in SPAN for y in SPAN])


def send(value, moves):
    return lax.ppermute(value, BOTH, moves)


def spread_corner(block, x, z, y):
    e = jnp.where((x == 0) & (z == 0) & (y < 2), block, 0.0)
    e = e + send(e, along_x([(0, 1)]))
    e = e + send(e, along_x([(0, 3), (1, 2)]))
    e = e + send(e, pairs(along_z([(0, 1)])))
    e = e + send(e, pairs(along_z([(0, 3), (1, 2)])))
    f = send(e, pairs(along_y([(0, 1), (1, 0)])))
    two = jnp.where(y == 0, jnp.stack([e, f]), jnp.stack([f, e]))
    two = jnp.where(y < 2, two, 0.0)
    return two + send(two, pairs(along_y([(0, 3), (1, 2)])))


def spread_rows(units, core, z, y):
    first = core == 0
    lone = lax.dynamic_slice_in_dim(units, 2 + 2 * core, 2, 0)
    split_y = along_y([(0, 3), (1, 2)], cores=(1,), zs=(0,))
    r1 = send(lone, pairs(along_z([(0, 1)], cores=(0,), ys=(0, 1)) + split_y))
    r2 = send(units[6:8], pairs(along_z([(0, 3)], cores=(0,), ys=(0, 1)) + split_y))
    r3 = send(units[4:6], pairs(along_z([(0, 2)], cores=(0,), ys=(0, 1))))
    kept = jnp.where(first, z == 0, y < 2)
    r_all = r1 + r2 + r3
    x0 = jnp.where(kept, units[0:2], jnp.where(first, r_all, r1))
    x1 = jnp.where(first, x0, jnp.where(kept, units[2:4], r2))
    own = jnp.concatenate([x0, x1])
    up = [(a, a + 1) for a in SPAN]
    down = [(a, a - 1) for a in SPAN]
    bp = send(own, pairs(along_y([(0, 1), (1, 2)], cores=(0,)) + along_z([(0, 1)], cores=(1,))))
    bm = send(own, pairs(along_y([(0, 3), (1, 0)], cores=(0,)) + along_z([(0, 3)], cores=(1,))))
    rp = send(bp[0:2], pairs(along_y([(1, 2), (2, 3)], cores=(0,)) + along_z([(1, 2)], cores=(1,))))
    rm = send(bm[2:4], pairs(along_z([(3, 2)], cores=(1,))))
    at = jnp.where(first, y, z)
    g0 = jnp.where(
        first,
        lax.select_n(at, own[0:2], bp[0:2], rp, bm[0:2]),
        lax.select_n(at, own[0:2], bp[0:2], rp, bm[0:2]),
    )
    g1 = lax.select_n(
        jnp.where(first, at, at + 4),
        bm[2:4], own[2:4], bp[2:4], rp,
        own[2:4], bp[2:4], rm, bm[2:4],
    )
    g = jnp.concatenate([g0, g1])
    ahead = pairs(along_z(up, cores=(0,)) + along_y(up, cores=(1,)))
    back = pairs(along_z(down, cores=(0,)) + along_y(down, cores=(1,)))
    gp = send(g, ahead)
    gm = send(g, back)
    return g, gp, gm, send(gp[0:2], ahead), send(gm[2:4], back)


def local(kernel):
    row = lax.axis_index("row")
    col = lax.axis_index("col")
    x, core, z, y = row // 2, row % 2, col // 4, col % 4
    place = jnp.stack([row, col, core, z, y]).astype(jnp.int32)
    m = kernel.reshape(16 * NB, 8, NB)
    top = m[0:NB]
    mine = spread_corner(top[:, 0, :], x, z, y)
    other = send(mine, SWAP)
    lower, inverse = factor_corner(place[2:3], mine, other)
    pieces = spread_rows(m[:, 0, :].reshape(8, TR, NB), core, z, y)
    c = jnp.where(
        x == 0,
        top,
        send(top, along_x([(0, 1)])) + send(top, along_x([(0, 3)])) + send(top, along_x([(0, 2)])),
    )
    result = update_trailing(place, lower, inverse, *pieces, c, send(c, SWAP), m)
    return result.reshape(kernel.shape)


def solution(mesh):
    placed = P(None, "row", None, None, "col", None)
    return jax.shard_map(local, mesh=mesh, in_specs=(placed,), out_specs=placed, check_vma=False)
```

time: 544 us -> 99.3 us (0.18)
  the two profiles are of different devices: /device:TPU:15 before, /device:TPU:59 now
where the time goes in v1:
time: 99.3 us; the launch traced here: 98.8 us
  waiting for transfers between devices  35.6 us (36%)
  starting transfers between devices  27.2 us (27%)
  Pallas kernels  18.5 us (19%)
  local copies, waits for them, and re-layouts  15.2 us (15%)
  other arithmetic  1.83 us (2%)
    ppermute x22, waiting for transfers between devices, send(): return lax.ppermute(value, BOTH, moves)  35.6 us
    ppermute x22, starting transfers between devices, send(): return lax.ppermute(value, BOTH, moves)  27.2 us
    pallas_call x1, Pallas kernels, update_trailing(): pl.pallas_call(trailing_kernel, grid=(rows // TR,), out_shape=jax.ShapeDt...  10.2 us
    pallas_call x1, Pallas kernels, factor_corner(): pl.pallas_call(factor_kernel, out_shape=(jax.ShapeDtypeStruct((W2, W2), F...  8.3 us
    slice x1, local copies, waits for them, and re-layouts, spread_rows(): x0 = jnp.where(kept, units[0:2], jnp.where(first, r_all, r1))  4.01 us
    slice x1, local copies, waits for them, and re-layouts, local(): pieces = spread_rows(m[:, 0, :].reshape(8, TR, NB), core, z, y)  3.75 us
    unnamed x2, local copies, waits for them, and re-layouts  3.38 us
  transfers between devices with their start and end apart: 22, of which 6 were waited for; matrix products, arithmetic and copies ran while one was open for 10% of the time, Pallas kernels for 8%

profile of v1, /device:TPU:59, one launch (start us, length us, event | category | flops | bytes accessed | tf_op | source)
XLA Modules:
  0.0 98.8 jit_solution(12001926898828360080)
XLA Ops:
  0.0 3.8 %slice.85 = f32[2048,1,128]{2,1,0:T(1,128)S(1)} slice(f32[2048,8,128]{2,1,0:T(8,128)} %bitcast.28), slice={[0:2048], [0:1], [0:128]} | slice | bytes 2097152 | tf_op jit(solution)/shard_map/slice | solution.py:343
  4.5 4.0 %fusion.3 = (f32[512,1,128]{2,1,0:T(1,128)S(1)}, f32[512,1,128]{2,1,0:T(1,128)S(1)}, f32[512,1,128]{2,1,0:T(1,128)S(1)}, f32[512,1,128]{2,1,0:T(1,128)S(1)}) fusion(f32[2048,8,128]{2,1,0:T(8,128)} %bitcast.29), kind=kLoop, calls=%fused_computation.14 | loop fusion | bytes 2097152 | tf_op jit(solution)/shard_map/slice | solution.py:305
  10.8 1.3 %collective-permute-start.10 = (f32[4,256,128]{2,1,0:T(8,128)S(1)}, f32[4,256,128]{2,1,0:T(8,128)S(1)}, u32[]{:S(2)}, u32[]{:S(2)}) collective-permute-start(f32[4,256,128]{2,1,0:T(8,128)S(1)} %pad_maximum_fusion), channel_id=1, source_target_pairs={{0,1},{4,5},{8,9},{12,13},{32,33},{36,37},{40,41},{44,45},{64,65},... | collective-permute-start | bytes 1572872 | tf_op jit(solution)/shard_map/ppermute | solution.py:281
  13.2 1.3 %collective-permute-start = (f32[128,128]{1,0:T(8,128)S(1)}, f32[128,128]{1,0:T(8,128)S(1)}, u32[]{:S(2)}, u32[]{:S(2)}) collective-permute-start(f32[128,128]{1,0:T(8,128)S(1)} %bitcast.38), channel_id=1, source_target_pairs={{0,32},{1,33},{2,34},{3,35},{4,36},{5,37},{6,38},{7,39},{8,40},{9,... | collective-permute-start | bytes 196616 | tf_op jit(solution)/shard_map/ppermute | solution.py:281
  14.5 4.0 %collective-permute-done = f32[128,128]{1,0:T(8,128)S(1)} collective-permute-done((f32[128,128]{1,0:T(8,128)S(1)}, f32[128,128]{1,0:T(8,128)S(1)}, u32[]{:S(2)}, u32[]{:S(2)}) %collective-permute-start) | collective-permute-done | bytes 65568 | tf_op jit(solution)/shard_map/ppermute | solution.py:281
  18.5 1.3 %collective-permute-start.1 = (f32[128,128]{1,0:T(8,128)S(1)}, f32[128,128]{1,0:T(8,128)S(1)}, u32[]{:S(2)}, u32[]{:S(2)}) collective-permute-start(f32[128,128]{1,0:T(8,128)S(1)} %add.49), channel_id=1, source_target_pairs={{0,96},{1,97},{2,98},{3,99},{4,100},{5,101},{6,102},{7,103},{8,104... | collective-permute-start | bytes 196616 | tf_op jit(solution)/shard_map/ppermute | solution.py:281
  21.3 6.0 %collective-permute-done.10 = f32[4,256,128]{2,1,0:T(8,128)S(1)} collective-permute-done((f32[4,256,128]{2,1,0:T(8,128)S(1)}, f32[4,256,128]{2,1,0:T(8,128)S(1)}, u32[]{:S(2)}, u32[]{:S(2)}) %collective-permute-start.10) | collective-permute-done | bytes 524320 | tf_op jit(solution)/shard_map/ppermute | solution.py:281
  28.0 1.3 %collective-permute-start.11 = (f32[2,256,128]{2,1,0:T(8,128)}, f32[2,256,128]{2,1,0:T(8,128)S(1)}, u32[]{:S(2)}, u32[]{:S(2)}) collective-permute-start(f32[2,256,128]{2,1,0:T(8,128)} %slice.89), channel_id=1, source_target_pairs={{1,2},{5,6},{9,10},{13,14},{33,34},{37,38},{41,42},{45,46},{65,66}... | collective-permute-start | bytes 786440 | tf_op jit(solution)/shard_map/ppermute | solution.py:281
  29.3 1.3 %collective-permute-start.2 = (f32[128,128]{1,0:T(8,128)S(1)}, f32[128,128]{1,0:T(8,128)S(1)}, u32[]{:S(2)}, u32[]{:S(2)}) collective-permute-start(f32[128,128]{1,0:T(8,128)S(1)} %add.50), channel_id=1, source_target_pairs={{0,4},{1,5},{2,6},{3,7},{16,20},{17,21},{18,22},{19,23},{32,36},{3... | collective-permute-start | bytes 196616 | tf_op jit(solution)/shard_map/ppermute | solution.py:281
  30.6 3.7 %collective-permute-done.2 = f32[128,128]{1,0:T(8,128)S(1)} collective-permute-done((f32[128,128]{1,0:T(8,128)S(1)}, f32[128,128]{1,0:T(8,128)S(1)}, u32[]{:S(2)}, u32[]{:S(2)}) %collective-permute-start.2) | collective-permute-done | bytes 65568 | tf_op jit(solution)/shard_map/ppermute | solution.py:281
  34.3 1.3 %collective-permute-start.3 = (f32[128,128]{1,0:T(8,128)S(1)}, f32[128,128]{1,0:T(8,128)S(1)}, u32[]{:S(2)}, u32[]{:S(2)}) collective-permute-start(f32[128,128]{1,0:T(8,128)S(1)} %add.51), channel_id=1, source_target_pairs={{0,12},{1,13},{2,14},{3,15},{16,28},{17,29},{18,30},{19,31},{32,44... | collective-permute-start | bytes 196616 | tf_op jit(solution)/shard_map/ppermute | solution.py:281
  36.3 1.5 %collective-permute-start.19 = (f32[128,8,128]{2,1,0:T(8,128)S(1)}, f32[128,8,128]{2,1,0:T(8,128)}, u32[]{:S(2)}, u32[]{:S(2)}) collective-permute-start(f32[128,8,128]{2,1,0:T(8,128)S(1)} %slice_bitcast_fusion), channel_id=1, source_target_pairs={{0,96},{1,97},{2,98},{3,99},{4,100},{5,101},{6,102},{7,103},{8,104... | collective-permute-start | bytes 1572872 | tf_op jit(solution)/shard_map/ppermute | solution.py:281
  37.8 1.3 %collective-permute-start.18 = (f32[128,8,128]{2,1,0:T(8,128)S(1)}, f32[128,8,128]{2,1,0:T(8,128)}, u32[]{:S(2)}, u32[]{:S(2)}) collective-permute-start(f32[128,8,128]{2,1,0:T(8,128)S(1)} %slice_bitcast_fusion), channel_id=1, source_target_pairs={{0,32},{1,33},{2,34},{3,35},{4,36},{5,37},{6,38},{7,39},{8,40},{9,... | collective-permute-start | bytes 1572872 | tf_op jit(solution)/shard_map/ppermute | solution.py:281
  40.1 2.7 %collective-permute-start.14 = (f32[4,256,128]{2,1,0:T(8,128)S(1)}, f32[4,256,128]{2,1,0:T(8,128)S(1)}, u32[]{:S(2)}, u32[]{:S(2)}) collective-permute-start(f32[4,256,128]{2,1,0:T(8,128)S(1)} %pad_maximum_fusion.1.g_ref), channel_id=1, source_target_pairs={{0,4},{1,5},{2,6},{3,7},{32,36},{33,37},{34,38},{35,39},{64,68},{6... | collective-permute-start | bytes 1572872 | tf_op jit(solution)/shard_map/ppermute | solution.py:281
  42.8 18.7 %collective-permute-done.18 = f32[128,8,128]{2,1,0:T(8,128)} collective-permute-done((f32[128,8,128]{2,1,0:T(8,128)S(1)}, f32[128,8,128]{2,1,0:T(8,128)}, u32[]{:S(2)}, u32[]{:S(2)}) %collective-permute-start.18) | collective-permute-done | bytes 524320 | tf_op jit(solution)/shard_map/ppermute | solution.py:281
  61.5 1.5 %add_select_fusion.cmine_ref = f32[128,8,128]{2,1,0:T(8,128)S(1)} fusion(f32[128,8,128]{2,1,0:T(8,128)S(1)} %collective-permute-done.20, f32[128,8,128]{2,1,0:T(8,128)} %collective-permute-done.18, f32[128,8,128]{2,1,0:T(8,128)} %collective-permute-done.19, pred[]{:T(512)S(6)} %eq.18, f32[16,1,128,8,1,128]{5,3,2,4,1,0:T(8,128)} %bitcast.31), kind=kLoop, calls=%fused_computation.3 | loop fusion | flops 393216 | bytes 2621441 | tf_op jit(solution)/shard_map/jit(_where)/select_n | solution.py:344
  63.0 3.3 %collective-permute-start.21 = (f32[128,8,128]{2,1,0:T(8,128)S(1)}, f32[128,8,128]{2,1,0:T(8,128)S(1)}, u32[]{:S(2)}, u32[]{:S(2)}) collective-permute-start(f32[128,8,128]{2,1,0:T(8,128)S(1)} %add_select_fusion.cmine_ref), channel_id=1, source_target_pairs={{0,16},{1,17},{2,18},{3,19},{4,20},{5,21},{6,22},{7,23},{8,24},{9,... | collective-permute-start | bytes 1572872 | tf_op jit(solution)/shard_map/ppermute | solution.py:281
  66.3 1.3 %collective-permute-start.5 = (f32[2,128,128]{2,1,0:T(8,128)S(1)}, f32[2,128,128]{2,1,0:T(8,128)S(1)}, u32[]{:S(2)}, u32[]{:S(2)}) collective-permute-start(f32[2,128,128]{2,1,0:T(8,128)S(1)} %fusion.2), channel_id=1, source_target_pairs={{0,3},{4,7},{8,11},{12,15},{16,19},{20,23},{24,27},{28,31},{32,35}... | collective-permute-start | bytes 393224 | tf_op jit(solution)/shard_map/ppermute | solution.py:281
  69.1 3.3 %collective-permute-start.16 = (f32[2,256,128]{2,1,0:T(8,128)}, f32[2,256,128]{2,1,0:T(8,128)S(1)}, u32[]{:S(2)}, u32[]{:S(2)}) collective-permute-start(f32[2,256,128]{2,1,0:T(8,128)} %slice.93), channel_id=1, source_target_pairs={{0,4},{1,5},{2,6},{3,7},{32,36},{33,37},{34,38},{35,39},{64,68},{6... | collective-permute-start | bytes 786440 | tf_op jit(solution)/shard_map/ppermute | solution.py:281
  72.3 2.2 %collective-permute-done.5 = f32[2,128,128]{2,1,0:T(8,128)S(1)} collective-permute-done((f32[2,128,128]{2,1,0:T(8,128)S(1)}, f32[2,128,128]{2,1,0:T(8,128)S(1)}, u32[]{:S(2)}, u32[]{:S(2)}) %collective-permute-start.5) | collective-permute-done | bytes 131104 | tf_op jit(solution)/shard_map/ppermute | solution.py:281
  74.5 1.3 %collective-permute-start.6 = (f32[2,128,128]{2,1,0:T(8,128)S(1)}, f32[2,128,128]{2,1,0:T(8,128)S(1)}, u32[]{:S(2)}, u32[]{:S(2)}) collective-permute-start(f32[2,128,128]{2,1,0:T(8,128)S(1)} %fusion.4.mine_ref), channel_id=1, source_target_pairs={{0,16},{1,17},{2,18},{3,19},{4,20},{5,21},{6,22},{7,23},{8,24},{9,... | collective-permute-start | bytes 393224 | tf_op jit(solution)/shard_map/ppermute | solution.py:281
  76.8 8.3 %corner_factor.1 = (f32[256,256]{1,0:T(8,128)S(1)}, f32[256,256]{1,0:T(8,128)S(1)}) custom-call(s32[1]{0:T(128)} %bitcast.2.where_ref, f32[2,128,128]{2,1,0:T(8,128)S(1)} %fusion.4.mine_ref, f32[2,128,128]{2,1,0:T(8,128)S(1)} %collective-permute-done.6.other_ref), custom_call_target="tpu_custom_call" | custom-call | flops 20000000 | bytes 1000000 | tf_op jit(solution)/shard_map/corner_factor/pallas_call | solution.py:115
  85.1 3.4 %copy-done = f32[16,1,128,8,1,128]{5,4,3,2,1,0:T(1,128)S(1)} copy-done((f32[16,1,128,8,1,128]{5,4,3,2,1,0:T(1,128)S(1)}, f32[16,1,128,8,1,128]{5,4,3,2,1,0:T(1,128)}, u32[]{:S(2)}) %copy-start) | copy-done | bytes 8388632
  88.5 10.2 %trailing_update.1 = f32[2048,8,128]{2,1,0:T(8,128)} custom-call(s32[5]{0:T(128)S(1)} %stack.37.place_ref, f32[256,256]{1,0:T(8,128)S(1)} %get-tuple-element.7.lower_ref, f32[256,256]{1,0:T(8,128)S(1)} %get-tuple-element.8.inverse_ref, f32[4,256,128]{2,1,0:T(8,128)S(1)} %pad_maximum_fusion.1.g_ref, f32[4,256,128]{2,1,0:T(8,128)S(1)} %collective-permute-done.14.gp_ref, ...), custom_call_target="tpu_custom_call" | custom-call | flops 4000000000 | bytes 20000000 | tf_op jit(solution)/shard_map/trailing_update/pallas_call | solution.py:221
  (45 shorter events, 10.2 us)
Async XLA Ops:
  3.8 6.1 %collective-permute-start.7 = (f32[2,256,128]{2,1,0:T(8,128)S(1)}, f32[2,256,128]{2,1,0:T(8,128)S(1)}, u32[]{:S(2)}, u32[]{:S(2)}) collective-permute-start(f32[2,256,128]{2,1,0:T(8,128)S(1)} %constant_dynamic-slice_fusion), channel_id=1, source_target_pairs={{0,4},{1,5},{32,36},{33,37},{64,68},{65,69},{96,100},{97,101},{16,... | collective-permute-start | bytes 786440 | tf_op jit(solution)/shard_map/ppermute | solution.py:281
  8.5 1.4 %collective-permute-start.9 = (f32[2,256,128]{2,1,0:T(8,128)S(1)}, f32[2,256,128]{2,1,0:T(8,128)S(1)}, u32[]{:S(2)}, u32[]{:S(2)}) collective-permute-start(f32[2,256,128]{2,1,0:T(8,128)S(1)} %bitcast.43), channel_id=1, source_target_pairs={{0,8},{1,9},{32,40},{33,41},{64,72},{65,73},{96,104},{97,105}} | collective-permute-start | bytes 786440 | tf_op jit(solution)/shard_map/ppermute | solution.py:281
  9.2 0.8 collective-permute-start.8
  10.1 9.8 %collective-permute-start.12 = (f32[4,256,128]{2,1,0:T(8,128)S(1)}, f32[4,256,128]{2,1,0:T(8,128)S(1)}, u32[]{:S(2)}, u32[]{:S(2)}) collective-permute-start(f32[4,256,128]{2,1,0:T(8,128)S(1)} %pad_maximum_fusion), channel_id=1, source_target_pairs={{0,3},{4,7},{8,11},{12,15},{32,35},{36,39},{40,43},{44,47},{64,67}... | collective-permute-start | bytes 1572872 | tf_op jit(solution)/shard_map/ppermute | solution.py:281
  10.8 16.5 %collective-permute-start.10 = (f32[4,256,128]{2,1,0:T(8,128)S(1)}, f32[4,256,128]{2,1,0:T(8,128)S(1)}, u32[]{:S(2)}, u32[]{:S(2)}) collective-permute-start(f32[4,256,128]{2,1,0:T(8,128)S(1)} %pad_maximum_fusion), channel_id=1, source_target_pairs={{0,1},{4,5},{8,9},{12,13},{32,33},{36,37},{40,41},{44,45},{64,65},... | collective-permute-start | bytes 1572872 | tf_op jit(solution)/shard_map/ppermute | solution.py:281
  13.2 5.3 %collective-permute-start = (f32[128,128]{1,0:T(8,128)S(1)}, f32[128,128]{1,0:T(8,128)S(1)}, u32[]{:S(2)}, u32[]{:S(2)}) collective-permute-start(f32[128,128]{1,0:T(8,128)S(1)} %bitcast.38), channel_id=1, source_target_pairs={{0,32},{1,33},{2,34},{3,35},{4,36},{5,37},{6,38},{7,39},{8,40},{9,... | collective-permute-start | bytes 196616 | tf_op jit(solution)/shard_map/ppermute | solution.py:281
  18.5 10.7 %collective-permute-start.1 = (f32[128,128]{1,0:T(8,128)S(1)}, f32[128,128]{1,0:T(8,128)S(1)}, u32[]{:S(2)}, u32[]{:S(2)}) collective-permute-start(f32[128,128]{1,0:T(8,128)S(1)} %add.49), channel_id=1, source_target_pairs={{0,96},{1,97},{2,98},{3,99},{4,100},{5,101},{6,102},{7,103},{8,104... | collective-permute-start | bytes 196616 | tf_op jit(solution)/shard_map/ppermute | solution.py:281
  20.6 18.6 %collective-permute-start.13 = (f32[2,256,128]{2,1,0:T(8,128)}, f32[2,256,128]{2,1,0:T(8,128)S(1)}, u32[]{:S(2)}, u32[]{:S(2)}) collective-permute-start(f32[2,256,128]{2,1,0:T(8,128)} %slice.91), channel_id=1, source_target_pairs={{28,24},{29,25},{30,26},{31,27},{60,56},{61,57},{62,58},{63,59},{9... | collective-permute-start | bytes 786440 | tf_op jit(solution)/shard_map/ppermute | solution.py:281
  28.0 11.9 %collective-permute-start.11 = (f32[2,256,128]{2,1,0:T(8,128)}, f32[2,256,128]{2,1,0:T(8,128)S(1)}, u32[]{:S(2)}, u32[]{:S(2)}) collective-permute-start(f32[2,256,128]{2,1,0:T(8,128)} %slice.89), channel_id=1, source_target_pairs={{1,2},{5,6},{9,10},{13,14},{33,34},{37,38},{41,42},{45,46},{65,66}... | collective-permute-start | bytes 786440 | tf_op jit(solution)/shard_map/ppermute | solution.py:281
  29.3 5.0 %collective-permute-start.2 = (f32[128,128]{1,0:T(8,128)S(1)}, f32[128,128]{1,0:T(8,128)S(1)}, u32[]{:S(2)}, u32[]{:S(2)}) collective-permute-start(f32[128,128]{1,0:T(8,128)S(1)} %add.50), channel_id=1, source_target_pairs={{0,4},{1,5},{2,6},{3,7},{16,20},{17,21},{18,22},{19,23},{32,36},{3... | collective-permute-start | bytes 196616 | tf_op jit(solution)/shard_map/ppermute | solution.py:281
  34.3 3.5 %collective-permute-start.3 = (f32[128,128]{1,0:T(8,128)S(1)}, f32[128,128]{1,0:T(8,128)S(1)}, u32[]{:S(2)}, u32[]{:S(2)}) collective-permute-start(f32[128,128]{1,0:T(8,128)S(1)} %add.51), channel_id=1, source_target_pairs={{0,12},{1,13},{2,14},{3,15},{16,28},{17,29},{18,30},{19,31},{32,44... | collective-permute-start | bytes 196616 | tf_op jit(solution)/shard_map/ppermute | solution.py:281
  35.6 4.5 %collective-permute-start.20 = (f32[128,8,128]{2,1,0:T(8,128)S(1)}, f32[128,8,128]{2,1,0:T(8,128)S(1)}, u32[]{:S(2)}, u32[]{:S(2)}) collective-permute-start(f32[128,8,128]{2,1,0:T(8,128)S(1)} %slice_bitcast_fusion), channel_id=1, source_target_pairs={{0,64},{1,65},{2,66},{3,67},{4,68},{5,69},{6,70},{7,71},{8,72},{9,... | collective-permute-start | bytes 1572872 | tf_op jit(solution)/shard_map/ppermute | solution.py:281
  36.3 6.4 %collective-permute-start.19 = (f32[128,8,128]{2,1,0:T(8,128)S(1)}, f32[128,8,128]{2,1,0:T(8,128)}, u32[]{:S(2)}, u32[]{:S(2)}) collective-permute-start(f32[128,8,128]{2,1,0:T(8,128)S(1)} %slice_bitcast_fusion), channel_id=1, source_target_pairs={{0,96},{1,97},{2,98},{3,99},{4,100},{5,101},{6,102},{7,103},{8,104... | collective-permute-start | bytes 1572872 | tf_op jit(solution)/shard_map/ppermute | solution.py:281
  37.8 23.7 %collective-permute-start.18 = (f32[128,8,128]{2,1,0:T(8,128)S(1)}, f32[128,8,128]{2,1,0:T(8,128)}, u32[]{:S(2)}, u32[]{:S(2)}) collective-permute-start(f32[128,8,128]{2,1,0:T(8,128)S(1)} %slice_bitcast_fusion), channel_id=1, source_target_pairs={{0,32},{1,33},{2,34},{3,35},{4,36},{5,37},{6,38},{7,39},{8,40},{9,... | collective-permute-start | bytes 1572872 | tf_op jit(solution)/shard_map/ppermute | solution.py:281
  39.2 27.1 %collective-permute-start.4 = (f32[128,128]{1,0:T(8,128)S(1)}, f32[128,128]{1,0:T(8,128)S(1)}, u32[]{:S(2)}, u32[]{:S(2)}) collective-permute-start(f32[128,128]{1,0:T(8,128)S(1)} %add.52), channel_id=1, source_target_pairs={{0,1},{4,5},{8,9},{12,13},{16,17},{20,21},{24,25},{28,29},{32,33},... | collective-permute-start | bytes 196616 | tf_op jit(solution)/shard_map/ppermute | solution.py:281
  40.0 27.6 %collective-permute-start.15 = (f32[4,256,128]{2,1,0:T(8,128)S(1)}, f32[4,256,128]{2,1,0:T(8,128)S(1)}, u32[]{:S(2)}, u32[]{:S(2)}) collective-permute-start(f32[4,256,128]{2,1,0:T(8,128)S(1)} %pad_maximum_fusion.1.g_ref), channel_id=1, source_target_pairs={{0,12},{1,13},{2,14},{3,15},{32,44},{33,45},{34,46},{35,47},{64,76... | collective-permute-start | bytes 1572872 | tf_op jit(solution)/shard_map/ppermute | solution.py:281
  40.1 28.2 %collective-permute-start.14 = (f32[4,256,128]{2,1,0:T(8,128)S(1)}, f32[4,256,128]{2,1,0:T(8,128)S(1)}, u32[]{:S(2)}, u32[]{:S(2)}) collective-permute-start(f32[4,256,128]{2,1,0:T(8,128)S(1)} %pad_maximum_fusion.1.g_ref), channel_id=1, source_target_pairs={{0,4},{1,5},{2,6},{3,7},{32,36},{33,37},{34,38},{35,39},{64,68},{6... | collective-permute-start | bytes 1572872 | tf_op jit(solution)/shard_map/ppermute | solution.py:281
  63.0 22.1 %collective-permute-start.21 = (f32[128,8,128]{2,1,0:T(8,128)S(1)}, f32[128,8,128]{2,1,0:T(8,128)S(1)}, u32[]{:S(2)}, u32[]{:S(2)}) collective-permute-start(f32[128,8,128]{2,1,0:T(8,128)S(1)} %add_select_fusion.cmine_ref), channel_id=1, source_target_pairs={{0,16},{1,17},{2,18},{3,19},{4,20},{5,21},{6,22},{7,23},{8,24},{9,... | collective-permute-start | bytes 1572872 | tf_op jit(solution)/shard_map/ppermute | solution.py:281
  66.3 8.2 %collective-permute-start.5 = (f32[2,128,128]{2,1,0:T(8,128)S(1)}, f32[2,128,128]{2,1,0:T(8,128)S(1)}, u32[]{:S(2)}, u32[]{:S(2)}) collective-permute-start(f32[2,128,128]{2,1,0:T(8,128)S(1)} %fusion.2), channel_id=1, source_target_pairs={{0,3},{4,7},{8,11},{12,15},{16,19},{20,23},{24,27},{28,31},{32,35}... | collective-permute-start | bytes 393224 | tf_op jit(solution)/shard_map/ppermute | solution.py:281
  68.3 16.8 %collective-permute-start.17 = (f32[2,256,128]{2,1,0:T(8,128)}, f32[2,256,128]{2,1,0:T(8,128)S(1)}, u32[]{:S(2)}, u32[]{:S(2)}) collective-permute-start(f32[2,256,128]{2,1,0:T(8,128)} %slice.94), channel_id=1, source_target_pairs={{0,12},{1,13},{2,14},{3,15},{32,44},{33,45},{34,46},{35,47},{64,76... | collective-permute-start | bytes 786440 | tf_op jit(solution)/shard_map/ppermute | solution.py:281
  69.1 16.1 %collective-permute-start.16 = (f32[2,256,128]{2,1,0:T(8,128)}, f32[2,256,128]{2,1,0:T(8,128)S(1)}, u32[]{:S(2)}, u32[]{:S(2)}) collective-permute-start(f32[2,256,128]{2,1,0:T(8,128)} %slice.93), channel_id=1, source_target_pairs={{0,4},{1,5},{2,6},{3,7},{32,36},{33,37},{34,38},{35,39},{64,68},{6... | collective-permute-start | bytes 786440 | tf_op jit(solution)/shard_map/ppermute | solution.py:281
  74.5 2.3 %collective-permute-start.6 = (f32[2,128,128]{2,1,0:T(8,128)S(1)}, f32[2,128,128]{2,1,0:T(8,128)S(1)}, u32[]{:S(2)}, u32[]{:S(2)}) collective-permute-start(f32[2,128,128]{2,1,0:T(8,128)S(1)} %fusion.4.mine_ref), channel_id=1, source_target_pairs={{0,16},{1,17},{2,18},{3,19},{4,20},{5,21},{6,22},{7,23},{8,24},{9,... | collective-permute-start | bytes 393224 | tf_op jit(solution)/shard_map/ppermute | solution.py:281
  85.1 3.4 %copy-start = (f32[16,1,128,8,1,128]{5,4,3,2,1,0:T(1,128)S(1)}, f32[16,1,128,8,1,128]{5,4,3,2,1,0:T(1,128)}, u32[]{:S(2)}) copy-start(f32[16,1,128,8,1,128]{5,4,3,2,1,0:T(1,128)} %param.1) | copy-start | bytes 25165828

commit v2 on v1

v2 whole, which is shorter than its diff:
```python
import jax
import jax.numpy as jnp
from jax import lax
from jax.experimental import pallas as pl
from jax.experimental.pallas import tpu as pltpu
from jax.sharding import PartitionSpec as P

F32 = jnp.float32
BF16 = jnp.bfloat16
BOTH = ("row", "col")
NB = 128
W2 = 2 * NB
TR = 256


def split2(x):
    high = x.astype(BF16)
    return high, (x - high.astype(F32)).astype(BF16)


def factor_kernel(where_ref, mine_ref, other_ref, lower_ref, inverse_ref, s_ref):
    core = where_ref[0]
    size, sub_rows, group = W2, 8, 32

    def place(first, second):
        s_ref[0:NB, 0:NB] = first[0]
        s_ref[NB:W2, 0:NB] = second[0]
        s_ref[0:NB, NB:W2] = second[0].T
        s_ref[NB:W2, NB:W2] = second[1]

    @pl.when(core == 0)
    def _():
        place(mine_ref, other_ref)

    @pl.when(core == 1)
    def _():
        place(other_ref, mine_ref)

    rows = lax.broadcasted_iota(jnp.int32, (size, size), 0)
    cols = lax.broadcasted_iota(jnp.int32, (size, size), 1)
    s_ref[:, size:] = jnp.where(rows == cols, 1.0, 0.0)
    sub = lax.broadcasted_iota(jnp.int32, (sub_rows, NB), 0)
    tiles = 3
    width = NB * tiles
    panels = group // sub_rows
    for o in range(0, size, group):
        lo = (o // NB) * NB
        r = [
            [
                s_ref[o + sub_rows * q : o + sub_rows * (q + 1), lo + NB * t : lo + NB * (t + 1)]
                for t in range(tiles)
            ]
            for q in range(panels)
        ]
        for p in range(panels):
            oo = o - lo + p * sub_rows
            c = [
                [jnp.broadcast_to(r[q][0][:, oo + j : oo + j + 1], (sub_rows, NB)) for j in range(sub_rows)]
                if q >= p
                else None
                for q in range(panels)
            ]
            b = [
                [
                    jnp.broadcast_to(c[p][j][i : i + 1, :], (sub_rows, NB)) if i >= j else None
                    for j in range(sub_rows)
                ]
                for i in range(sub_rows)
            ]
            scale = None
            for k in range(sub_rows):
                s = lax.rsqrt(b[k][k])
                scale = s if scale is None else jnp.where(sub >= k, s, scale)
                m = [None] * sub_rows
                for i in range(k + 1, sub_rows):
                    m[i] = b[i][k] * s
                for i in range(k + 1, sub_rows):
                    for j in range(k + 1, i + 1):
                        b[i][j] = b[i][j] - m[i] * m[j]
                u = [jnp.broadcast_to(r[p][t][k : k + 1, :], (sub_rows, NB)) * s for t in range(tiles)]
                for q in range(p, panels):
                    mult = c[q][k] * s
                    for j in range(k + 1, sub_rows):
                        c[q][j] = c[q][j] - mult * m[j]
                    if q == p:
                        if k == sub_rows - 1:
                            continue
                        mult = jnp.where(sub > k, mult, 0.0)
                    r[q] = [r[q][t] - mult * u[t] for t in range(tiles)]
            for t in range(tiles):
                s_ref[
                    o + sub_rows * p : o + sub_rows * (p + 1), lo + NB * t : lo + NB * (t + 1)
                ] = r[p][t] * scale
        if o + group < size:
            lo2 = ((o + group) // NB) * NB
            uu = s_ref[o : o + group, lo2 : lo + width]
            left = size - lo2
            h = uu.astype(BF16).astype(F32)
            rest = uu - h
            mid = rest.astype(BF16).astype(F32)
            low = rest - mid
            lhs = jnp.concatenate([h, h, mid, h, low, mid], axis=0)[:, :left].astype(BF16)
            rhs = jnp.concatenate([h, mid, h, low, h, mid], axis=0).astype(BF16)
            update = lax.dot_general(lhs, rhs, (((0,), (0,)), ((), ())), preferred_element_type=F32)
            skip = o + group - lo2
            s_ref[o + group : size, lo2 : lo + width] = (
                s_ref[o + group : size, lo2 : lo + width] - update[skip:, :]
            )
    lower_ref[...] = jnp.where(cols >= rows, s_ref[:, 0:size], 0.0).T
    inverse_ref[...] = jnp.where(cols <= rows, s_ref[:, size:], 0.0)


def factor_corner(place, mine, other):
    vmem = pl.BlockSpec(memory_space=pltpu.VMEM)
    return pl.pallas_call(
        factor_kernel,
        out_shape=(jax.ShapeDtypeStruct((W2, W2), F32),) * 2,
        in_specs=[pl.BlockSpec(memory_space=pltpu.SMEM), vmem, vmem],
        out_specs=(vmem, vmem),
        scratch_shapes=[pltpu.VMEM((W2, 2 * W2), F32)],
        compiler_params=pltpu.CompilerParams(vmem_limit_bytes=8 * 1024 * 1024),
        cost_estimate=pl.CostEstimate(flops=8_000_000_000, bytes_accessed=1_000_000, transcendentals=256),
        name="corner_factor",
    )(place, mine, other)


STEPS = 8


def trailing_kernel(
    place_ref, lower_ref, inverse_ref, g_ref, gm_ref, gf_ref, gp_ref, columns_ref, m_ref,
    o_ref, a_ref, old_ref, new_ref, wc_ref, a_sems, m_sems, o_sems,
):
    row, col, core, z, y = (place_ref[n] for n in range(5))
    here = jnp.where(core == 0, z, y)
    pieces = [
        pltpu.make_async_copy(ref, a_ref.at[n], a_sems.at[n])
        for n, ref in enumerate((g_ref, gm_ref, gf_ref, gp_ref))
    ]
    for piece in pieces:
        piece.start()
    loads = [
        pltpu.make_async_copy(
            m_ref.at[s * TR : (s + 1) * TR], old_ref.at[s], m_sems.at[s]
        )
        for s in range(STEPS)
    ]
    for load in loads:
        load.start()

    inverse = inverse_ref[...]
    high, low = split2(inverse.T)
    lt = jnp.concatenate([high, low, high], axis=0)
    high, low = split2(inverse)
    lhs = jnp.concatenate([high, high, low], axis=1)
    for j in range(0, 8, 2):
        x = jnp.concatenate(
            [
                jnp.concatenate([columns_ref[n, :, jj, :] for n in range(2)], axis=0)
                for jj in (j, j + 1)
            ],
            axis=1,
        )
        xh, xl = split2(x)
        w = jnp.dot(lhs, jnp.concatenate([xh, xl, xh], axis=0), preferred_element_type=F32)
        wh, wl = split2(w)
        span = pl.ds(j * NB, W2)
        wc_ref[0:W2, span] = wh
        wc_ref[W2 : 2 * W2, span] = wl
        wc_ref[2 * W2 : 3 * W2, span] = wh
    for piece in pieces:
        piece.wait()

    stores = []
    for s in range(STEPS):
        half = s // 4
        slot0 = (jnp.where(core == 0, half, 3 * half) - here + 4) % 4
        slot1 = (jnp.where(core == 0, 2 + half, 1 + half) - here + 4) % 4
        a = jnp.concatenate([a_ref[slot0, s % 4], a_ref[slot1, s % 4]], axis=1)
        ah, al = split2(a)
        w = jnp.dot(jnp.concatenate([ah, ah, al], axis=1), lt, preferred_element_type=F32)
        wh, wl = split2(w)
        u = jnp.dot(jnp.concatenate([wh, wh, wl], axis=1), wc_ref[...], preferred_element_type=F32)
        loads[s].wait()
        new_ref[s] = old_ref[s] - u.reshape(TR, 8, NB)

        @pl.when(col == 0)
        def _():
            new_ref[s, :, 0, :] = w[:, 0:NB]

        @pl.when(col == 1)
        def _():
            new_ref[s, :, 0, :] = w[:, NB:W2]

        if s == 0:

            @pl.when(row < 2)
            def _():
                new_ref[s, 0:NB, :, :] = jnp.zeros((NB, 8, NB), F32)

                @pl.when(col < 2)
                def _():
                    new_ref[s, 0:NB, 0, :] = lower_ref[
                        pl.ds(pl.multiple_of(row * NB, NB), NB), pl.ds(pl.multiple_of(col * NB, NB), NB)
                    ]

        store = pltpu.make_async_copy(
            new_ref.at[s], o_ref.at[s * TR : (s + 1) * TR], o_sems.at[s]
        )
        store.start()
        stores.append(store)
    for store in stores:
        store.wait()


def update_trailing(place, lower, inverse, pieces, columns, m):
    anywhere = pl.BlockSpec(memory_space=pl.ANY)
    vmem = pl.BlockSpec(memory_space=pltpu.VMEM)
    return pl.pallas_call(
        trailing_kernel,
        out_shape=jax.ShapeDtypeStruct(m.shape, F32),
        in_specs=[pl.BlockSpec(memory_space=pltpu.SMEM), vmem, vmem] + [anywhere] * 4 + [vmem, anywhere],
        out_specs=anywhere,
        scratch_shapes=[
            pltpu.VMEM((4, 4, TR, NB), F32),
            pltpu.VMEM((STEPS, TR, 8, NB), F32),
            pltpu.VMEM((STEPS, TR, 8, NB), F32),
            pltpu.VMEM((3 * W2, 8 * NB), BF16),
            pltpu.SemaphoreType.DMA((4,)),
            pltpu.SemaphoreType.DMA((STEPS,)),
            pltpu.SemaphoreType.DMA((STEPS,)),
        ],
        compiler_params=pltpu.CompilerParams(vmem_limit_bytes=36 * 1024 * 1024),
        cost_estimate=pl.CostEstimate(flops=4_000_000_000, bytes_accessed=20_000_000, transcendentals=0),
        name="trailing_update",
    )(place, lower, inverse, *pieces, columns, m)


def device(x, core, z, y):
    return (x % 4 * 2 + core) * 16 + z % 4 * 4 + y % 4


def pairs(moves):
    return [(device(*a), device(*b)) for a, b in moves]


SPAN = range(4)
CORES = range(2)


def along_x(hops):
    return pairs(
        [((a, k, z, y), (b, k, z, y)) for a, b in hops for k in CORES for z in SPAN for y in SPAN]
    )


def along_z(hops, cores=CORES, ys=SPAN, xs=SPAN):
    return [((x, k, a, y), (x, k, b, y)) for a, b in hops for x in xs for k in cores for y in ys]


def along_y(hops, cores=CORES, zs=SPAN, xs=SPAN):
    return [((x, k, z, a), (x, k, z, b)) for a, b in hops for x in xs for k in cores for z in zs]


SWAP = pairs([((x, k, z, y), (x, 1 - k, z, y)) for x in SPAN for k in CORES for z in SPAN for y in SPAN])


def send(value, moves):
    return lax.ppermute(value, BOTH, moves)


def after(value, *others):
    return lax.optimization_barrier((value, *others))[0]


def extract_kernel(place_ref, m_ref, first_ref, second_ref, block_ref, top_ref, sems):
    x, z, y = (place_ref[n] for n in (5, 3, 4))
    top = pltpu.make_async_copy(m_ref.at[0:NB], top_ref, sems.at[9])
    block = pltpu.make_async_copy(m_ref.at[0:NB, 0, :], block_ref, sems.at[8])
    source = (z == 0) & (y < 2)
    corner = source & (x == 0)

    @pl.when(x == 0)
    def _():
        top.start()

    @pl.when(corner)
    def _():
        block.start()

    @pl.when(source)
    def _():
        copies = [
            pltpu.make_async_copy(m_ref.at[TR * n : TR * (n + 1), 0, :], ref.at[n % 4], sems.at[n])
            for n, ref in enumerate([first_ref] * 4 + [second_ref] * 4)
        ]
        for copy in copies:
            copy.start()
        for copy in copies:
            copy.wait()

    @pl.when(corner)
    def _():
        block.wait()

    @pl.when(jnp.logical_not(corner))
    def _():
        block_ref[...] = jnp.zeros((NB, NB), F32)

    @pl.when(x == 0)
    def _():
        top.wait()


def extract(place, m):
    anywhere = pl.BlockSpec(memory_space=pl.ANY)
    half = jax.ShapeDtypeStruct((4, TR, NB), F32)
    return pl.pallas_call(
        extract_kernel,
        out_shape=(half, half, jax.ShapeDtypeStruct((NB, NB), F32), jax.ShapeDtypeStruct((NB, 8, NB), F32)),
        in_specs=[pl.BlockSpec(memory_space=pltpu.SMEM), anywhere],
        out_specs=(anywhere, anywhere, pl.BlockSpec(memory_space=pltpu.VMEM), anywhere),
        scratch_shapes=[pltpu.SemaphoreType.DMA((10,))],
        compiler_params=pltpu.CompilerParams(vmem_limit_bytes=4 * 1024 * 1024),
        cost_estimate=pl.CostEstimate(flops=0, bytes_accessed=4_000_000, transcendentals=0),
        name="extract_panels",
    )(place, m)


def local(kernel):
    row = lax.axis_index("row")
    col = lax.axis_index("col")
    x, core, z, y = row // 2, row % 2, col // 4, col % 4
    place = jnp.stack([row, col, core, z, y, x]).astype(jnp.int32)
    m = kernel.reshape(16 * NB, 8, NB)
    m = pltpu.with_memory_space_constraint(m, pltpu.HBM)
    first, second, e, top = extract(place, m)

    plane = (0,)
    f = send(e, pairs(along_y([(0, 1), (1, 0)], xs=plane, zs=(0,))))

    lay_y = along_y([(0, 3), (1, 2)], cores=(1,), zs=(0,))
    r1 = send(second, pairs(along_z([(0, 1)], (0,), (0,)) + along_z([(0, 3)], (0,), (1,)) + lay_y))
    r2 = send(first, pairs(along_z([(0, 2)], (0,), (1,))))
    c1, c3 = (send(top, along_x([(0, to)])) for to in (1, 3))

    e = jnp.where(y == 0, jnp.stack([e, f]), jnp.stack([f, e]))
    e = jnp.where((x == 0) & (z == 0) & (y < 2), e, 0.0)
    e = e + send(e, pairs(along_z([(0, 1)], ys=(0, 1), xs=plane)))
    e = e + send(e, pairs(along_z([(0, 3), (1, 2)], ys=(0, 1), xs=plane)))
    e = e + send(e, pairs(along_y([(0, 3), (1, 2)], xs=plane)))

    kept = (z == 0) & jnp.where(core == 0, y == 0, y < 2)
    own = jnp.where(kept, first, r1 + r2)
    own = after(own, e)
    lines = [
        pairs(
            along_y([(0, d % 4)], (0,), (0, 1))
            + along_y([(1, (1 + d) % 4)], (0,), (2, 3))
            + along_z([(0, d % 4)], (1,))
        )
        for d in (1, 3, 2)
    ]
    b1, b3, b2 = (send(own, moves) for moves in lines)
    c2 = send(after(c1, c3, e), along_x([(1, 2)]))

    e = after(e, b3)
    e = e + send(e, along_x([(0, 3)]))
    mine = e + send(e, along_x([(0, 1), (3, 2)]))
    g = own + b1 + b2 + b3
    mine = after(mine, g)
    other = send(mine, SWAP)
    around = [
        pairs(
            along_z([(a, (a + d) % 4) for a in SPAN], (0,)) + along_y([(a, (a + d) % 4) for a in SPAN], (1,))
        )
        for d in (1, 3, 2)
    ]
    g1, g3, g2 = (send(g, moves) for moves in around)
    c = jnp.where(x == 0, top, c1 + c2 + c3)
    c = after(c, other)
    lower, inverse = factor_corner(place[2:3], mine, other)
    columns = jnp.stack([c, send(c, SWAP)])
    columns = jnp.where(core == 0, columns, columns[::-1])
    result = update_trailing(place, lower, inverse, (g, g3, g2, g1), columns, m)
    return result.reshape(kernel.shape)


def solution(mesh):
    placed = P(None, "row", None, None, "col", None)
    return jax.shard_map(local, mesh=mesh, in_specs=(placed,), out_specs=placed, check_vma=False)
```

time: 99.3 us -> 75.6 us (0.76)
  the two profiles are of different devices: /device:TPU:59 before, /device:TPU:15 now
where the time goes in v2:
time: 75.6 us; the launch traced here: 75.2 us
  starting transfers between devices  30.2 us (40%)
  Pallas kernels  22.3 us (29%)
  waiting for transfers between devices  20.5 us (27%)
  other arithmetic  1.67 us (2%)
    ppermute x19, starting transfers between devices, send(): return lax.ppermute(value, BOTH, moves)  30.2 us
    ppermute x19, waiting for transfers between devices, send(): return lax.ppermute(value, BOTH, moves)  20.5 us
    pallas_call x1, Pallas kernels, update_trailing(): pl.pallas_call(trailing_kernel, out_shape=jax.ShapeDtypeStruct(m.shape, F...  12.2 us
    pallas_call x1, Pallas kernels, factor_corner(): pl.pallas_call(factor_kernel, out_shape=(jax.ShapeDtypeStruct((W2, W2), F...  8.14 us
    pallas_call x1, Pallas kernels, extract(): pl.pallas_call(extract_kernel, out_shape=(half, half, jax.ShapeDtypeStruc...  1.92 us
  transfers between devices with their start and end apart: 19, of which 3 were waited for; matrix products, arithmetic and copies ran while one was open for 2% of the time, Pallas kernels for 11%

profile of v2, /device:TPU:15, one launch (start us, length us, event | category | flops | bytes accessed | tf_op | source)
XLA Modules:
  0.0 75.2 jit_solution(15325320544959196908)
XLA Ops:
  0.1 1.9 %extract_panels.1 = (f32[4,256,128]{2,1,0:T(8,128)S(1)}, f32[4,256,128]{2,1,0:T(8,128)S(1)}, f32[128,128]{1,0:T(8,128)S(1)}, f32[128,8,128]{2,1,0:T(8,128)S(1)}) custom-call(s32[6]{0:T(128)S(1)} %stack.50.place_ref, f32[2048,8,128]{2,1,0:T(8,128)} %bitcast.17), custom_call_target="tpu_custom_call" | custom-call | bytes 4000000 | tf_op jit(solution)/shard_map/extract_panels/pallas_call | solution.py:318
  2.0 0.7 collective-permute-start
  2.7 0.7 collective-permute-start.1
  3.4 2.0 %collective-permute-start.4 = (f32[4,256,128]{2,1,0:T(8,128)S(1)}, f32[4,256,128]{2,1,0:T(8,128)S(1)}, u32[]{:S(2)}, u32[]{:S(2)}) collective-permute-start(f32[4,256,128]{2,1,0:T(8,128)S(1)} %get-tuple-element.18), channel_id=1, source_target_pairs={{0,4},{32,36},{64,68},{96,100},{1,13},{33,45},{65,77},{97,109},{16... | collective-permute-start | bytes 1572872 | tf_op jit(solution)/shard_map/ppermute | solution.py:269
  5.4 0.7 collective-permute-start.5
  6.1 0.7 collective-permute-start.2
  6.9 0.7 collective-permute-start.3
  7.5 1.3 %collective-permute-start.16 = (f32[128,8,128]{2,1,0:T(8,128)S(1)}, f32[128,8,128]{2,1,0:T(8,128)S(1)}, u32[]{:S(2)}, u32[]{:S(2)}) collective-permute-start(f32[128,8,128]{2,1,0:T(8,128)S(1)} %get-tuple-element.24), channel_id=1, source_target_pairs={{0,96},{1,97},{2,98},{3,99},{4,100},{5,101},{6,102},{7,103},{8,104... | collective-permute-start | bytes 1572872 | tf_op jit(solution)/shard_map/ppermute | solution.py:269
  8.8 1.5 %collective-permute-start.15 = (f32[128,8,128]{2,1,0:T(8,128)S(1)}, f32[128,8,128]{2,1,0:T(8,128)}, u32[]{:S(2)}, u32[]{:S(2)}) collective-permute-start(f32[128,8,128]{2,1,0:T(8,128)S(1)} %get-tuple-element.24), channel_id=1, source_target_pairs={{0,32},{1,33},{2,34},{3,35},{4,36},{5,37},{6,38},{7,39},{8,40},{9,... | collective-permute-start | bytes 1572872 | tf_op jit(solution)/shard_map/ppermute | solution.py:269
  10.3 1.2 %collective-permute-done.4 = f32[4,256,128]{2,1,0:T(8,128)S(1)} collective-permute-done((f32[4,256,128]{2,1,0:T(8,128)S(1)}, f32[4,256,128]{2,1,0:T(8,128)S(1)}, u32[]{:S(2)}, u32[]{:S(2)}) %collective-permute-start.4) | collective-permute-done | bytes 524320 | tf_op jit(solution)/shard_map/ppermute | solution.py:269
  11.6 2.0 %collective-permute-start.6 = (f32[4,256,128]{2,1,0:T(8,128)S(1)}, f32[4,256,128]{2,1,0:T(8,128)S(1)}, u32[]{:S(2)}, u32[]{:S(2)}) collective-permute-start(f32[4,256,128]{2,1,0:T(8,128)S(1)} %add_select_fusion.1), channel_id=1, source_target_pairs={{0,3},{4,7},{32,35},{36,39},{64,67},{68,71},{96,99},{100,103},{9,8... | collective-permute-start | bytes 1572872 | tf_op jit(solution)/shard_map/ppermute | solution.py:269
  13.6 1.3 %collective-permute-start.10 = (f32[4,256,128]{2,1,0:T(8,128)S(1)}, f32[4,256,128]{2,1,0:T(8,128)S(1)}, u32[]{:S(2)}, u32[]{:S(2)}) collective-permute-start(f32[4,256,128]{2,1,0:T(8,128)S(1)} %add_select_fusion.1), channel_id=1, source_target_pairs={{0,2},{4,6},{32,34},{36,38},{64,66},{68,70},{96,98},{100,102},{9,1... | collective-permute-start | bytes 1572872 | tf_op jit(solution)/shard_map/ppermute | solution.py:269
  14.9 1.3 %collective-permute-start.9 = (f32[4,256,128]{2,1,0:T(8,128)S(1)}, f32[4,256,128]{2,1,0:T(8,128)S(1)}, u32[]{:S(2)}, u32[]{:S(2)}) collective-permute-start(f32[4,256,128]{2,1,0:T(8,128)S(1)} %add_select_fusion.1), channel_id=1, source_target_pairs={{0,1},{4,5},{32,33},{36,37},{64,65},{68,69},{96,97},{100,101},{9,1... | collective-permute-start | bytes 1572872 | tf_op jit(solution)/shard_map/ppermute | solution.py:269
  16.3 8.2 %collective-permute-done.16 = f32[128,8,128]{2,1,0:T(8,128)S(1)} collective-permute-done((f32[128,8,128]{2,1,0:T(8,128)S(1)}, f32[128,8,128]{2,1,0:T(8,128)S(1)}, u32[]{:S(2)}, u32[]{:S(2)}) %collective-permute-start.16) | collective-permute-done | bytes 524320 | tf_op jit(solution)/shard_map/ppermute | solution.py:269
  24.5 0.7 collective-permute-start.17
  25.2 1.3 %collective-permute-start.7 = (f32[2,128,128]{2,1,0:T(8,128)S(1)}, f32[2,128,128]{2,1,0:T(8,128)S(1)}, u32[]{:S(2)}, u32[]{:S(2)}) collective-permute-start(f32[2,128,128]{2,1,0:T(8,128)S(1)} %add.46), channel_id=1, source_target_pairs={{0,96},{1,97},{2,98},{3,99},{4,100},{5,101},{6,102},{7,103},{8,104... | collective-permute-start | bytes 393224 | tf_op jit(solution)/shard_map/ppermute | solution.py:269
  26.5 11.1 %collective-permute-done.7 = f32[2,128,128]{2,1,0:T(8,128)S(1)} collective-permute-done((f32[2,128,128]{2,1,0:T(8,128)S(1)}, f32[2,128,128]{2,1,0:T(8,128)S(1)}, u32[]{:S(2)}, u32[]{:S(2)}) %collective-permute-start.7) | collective-permute-done | bytes 131104 | tf_op jit(solution)/shard_map/ppermute | solution.py:269
  37.6 1.3 %collective-permute-start.8 = (f32[2,128,128]{2,1,0:T(8,128)S(1)}, f32[2,128,128]{2,1,0:T(8,128)S(1)}, u32[]{:S(2)}, u32[]{:S(2)}) collective-permute-start(f32[2,128,128]{2,1,0:T(8,128)S(1)} %add.48), channel_id=1, source_target_pairs={{0,32},{1,33},{2,34},{3,35},{4,36},{5,37},{6,38},{7,39},{8,40},{9,... | collective-permute-start | bytes 393224 | tf_op jit(solution)/shard_map/ppermute | solution.py:269
  39.0 0.4 collective-permute-start.14
  39.4 1.9 %collective-permute-start.12 = (f32[4,256,128]{2,1,0:T(8,128)S(1)}, f32[4,256,128]{2,1,0:T(8,128)S(1)}, u32[]{:S(2)}, u32[]{:S(2)}) collective-permute-start(f32[4,256,128]{2,1,0:T(8,128)S(1)} %add_add_fusion.g_ref), channel_id=1, source_target_pairs={{0,12},{1,13},{2,14},{3,15},{32,44},{33,45},{34,46},{35,47},{64,76... | collective-permute-start | bytes 1572872 | tf_op jit(solution)/shard_map/ppermute | solution.py:269
  41.3 11.8 %collective-permute-start.11 = (f32[2,128,128]{2,1,0:T(8,128)S(1)}, f32[2,128,128]{2,1,0:T(8,128)S(1)}, u32[]{:S(2)}, u32[]{:S(2)}) collective-permute-start(f32[2,128,128]{2,1,0:T(8,128)S(1)} %add.49.mine_ref), channel_id=1, source_target_pairs={{0,16},{1,17},{2,18},{3,19},{4,20},{5,21},{6,22},{7,23},{8,24},{9,... | collective-permute-start | bytes 393224 | tf_op jit(solution)/shard_map/ppermute | solution.py:269
  53.1 1.2 %add_select_fusion = f32[128,8,128]{2,1,0:T(8,128)S(1)} fusion(f32[128,8,128]{2,1,0:T(8,128)S(1)} %get-tuple-element.24, f32[128,8,128]{2,1,0:T(8,128)S(1)} %collective-permute-done.16, f32[128,8,128]{2,1,0:T(8,128)} %collective-permute-done.15, f32[128,8,128]{2,1,0:T(8,128)S(1)} %collective-permute-done.17, pred[]{:T(512)S(6)} %eq.19), kind=kLoop, calls=%fused_computation.2 | loop fusion | flops 393216 | bytes 2621441 | tf_op jit(solution)/shard_map/jit(_where)/select_n | solution.py:380
  54.5 8.1 %corner_factor.1 = (f32[256,256]{1,0:T(8,128)S(1)}, f32[256,256]{1,0:T(8,128)S(1)}) custom-call(s32[1]{0:T(128)} %bitcast.2.where_ref, f32[2,128,128]{2,1,0:T(8,128)S(1)} %add.49.mine_ref, f32[2,128,128]{2,1,0:T(8,128)S(1)} %collective-permute-done.11.other_ref), custom_call_target="tpu_custom_call" | custom-call | flops 8000000000 | bytes 1000000 | tf_op jit(solution)/shard_map/corner_factor/pallas_call | solution.py:115
  62.8 12.2 %trailing_update.1 = f32[2048,8,128]{2,1,0:T(8,128)} custom-call(s32[6]{0:T(128)S(1)} %stack.50.place_ref, f32[256,256]{1,0:T(8,128)S(1)} %get-tuple-element.22.lower_ref, f32[256,256]{1,0:T(8,128)S(1)} %get-tuple-element.23.inverse_ref, f32[4,256,128]{2,1,0:T(8,128)S(1)} %add_add_fusion.g_ref, f32[4,256,128]{2,1,0:T(8,128)S(1)} %collective-permute-done.12.gm_ref, ...), custom_call_target="tpu_custom_call" | custom-call | flops 4000000000 | bytes 20000000 | tf_op jit(solution)/shard_map/trailing_update/pallas_call | solution.py:219
  (29 shorter events, 0.7 us)
Async XLA Ops:
  2.0 0.7 collective-permute-start
  2.7 3.4 %collective-permute-start.1 = (f32[2,128,128]{2,1,0:T(8,128)S(1)}, f32[2,128,128]{2,1,0:T(8,128)S(1)}, u32[]{:S(2)}, u32[]{:S(2)}) collective-permute-start(f32[2,128,128]{2,1,0:T(8,128)S(1)} %fusion), channel_id=1, source_target_pairs={{0,4},{1,5},{16,20},{17,21}} | collective-permute-start | bytes 393224 | tf_op jit(solution)/shard_map/ppermute | solution.py:269
  3.4 8.1 %collective-permute-start.4 = (f32[4,256,128]{2,1,0:T(8,128)S(1)}, f32[4,256,128]{2,1,0:T(8,128)S(1)}, u32[]{:S(2)}, u32[]{:S(2)}) collective-permute-start(f32[4,256,128]{2,1,0:T(8,128)S(1)} %get-tuple-element.18), channel_id=1, source_target_pairs={{0,4},{32,36},{64,68},{96,100},{1,13},{33,45},{65,77},{97,109},{16... | collective-permute-start | bytes 1572872 | tf_op jit(solution)/shard_map/ppermute | solution.py:269
  5.4 6.1 %collective-permute-start.5 = (f32[4,256,128]{2,1,0:T(8,128)S(1)}, f32[4,256,128]{2,1,0:T(8,128)S(1)}, u32[]{:S(2)}, u32[]{:S(2)}) collective-permute-start(f32[4,256,128]{2,1,0:T(8,128)S(1)} %get-tuple-element.17), channel_id=1, source_target_pairs={{1,9},{33,41},{65,73},{97,105}} | collective-permute-start | bytes 1572872 | tf_op jit(solution)/shard_map/ppermute | solution.py:269
  6.1 0.7 collective-permute-start.2
  6.9 3.4 %collective-permute-start.3 = (f32[2,128,128]{2,1,0:T(8,128)S(1)}, f32[2,128,128]{2,1,0:T(8,128)S(1)}, u32[]{:S(2)}, u32[]{:S(2)}) collective-permute-start(f32[2,128,128]{2,1,0:T(8,128)S(1)} %fusion.2), channel_id=1, source_target_pairs={{0,3},{4,7},{8,11},{12,15},{16,19},{20,23},{24,27},{28,31},{1,2},{... | collective-permute-start | bytes 393224 | tf_op jit(solution)/shard_map/ppermute | solution.py:269
  7.5 16.9 %collective-permute-start.16 = (f32[128,8,128]{2,1,0:T(8,128)S(1)}, f32[128,8,128]{2,1,0:T(8,128)S(1)}, u32[]{:S(2)}, u32[]{:S(2)}) collective-permute-start(f32[128,8,128]{2,1,0:T(8,128)S(1)} %get-tuple-element.24), channel_id=1, source_target_pairs={{0,96},{1,97},{2,98},{3,99},{4,100},{5,101},{6,102},{7,103},{8,104... | collective-permute-start | bytes 1572872 | tf_op jit(solution)/shard_map/ppermute | solution.py:269
  8.8 15.6 %collective-permute-start.15 = (f32[128,8,128]{2,1,0:T(8,128)S(1)}, f32[128,8,128]{2,1,0:T(8,128)}, u32[]{:S(2)}, u32[]{:S(2)}) collective-permute-start(f32[128,8,128]{2,1,0:T(8,128)S(1)} %get-tuple-element.24), channel_id=1, source_target_pairs={{0,32},{1,33},{2,34},{3,35},{4,36},{5,37},{6,38},{7,39},{8,40},{9,... | collective-permute-start | bytes 1572872 | tf_op jit(solution)/shard_map/ppermute | solution.py:269
  11.6 13.6 %collective-permute-start.6 = (f32[4,256,128]{2,1,0:T(8,128)S(1)}, f32[4,256,128]{2,1,0:T(8,128)S(1)}, u32[]{:S(2)}, u32[]{:S(2)}) collective-permute-start(f32[4,256,128]{2,1,0:T(8,128)S(1)} %add_select_fusion.1), channel_id=1, source_target_pairs={{0,3},{4,7},{32,35},{36,39},{64,67},{68,71},{96,99},{100,103},{9,8... | collective-permute-start | bytes 1572872 | tf_op jit(solution)/shard_map/ppermute | solution.py:269
  13.6 25.3 %collective-permute-start.10 = (f32[4,256,128]{2,1,0:T(8,128)S(1)}, f32[4,256,128]{2,1,0:T(8,128)S(1)}, u32[]{:S(2)}, u32[]{:S(2)}) collective-permute-start(f32[4,256,128]{2,1,0:T(8,128)S(1)} %add_select_fusion.1), channel_id=1, source_target_pairs={{0,2},{4,6},{32,34},{36,38},{64,66},{68,70},{96,98},{100,102},{9,1... | collective-permute-start | bytes 1572872 | tf_op jit(solution)/shard_map/ppermute | solution.py:269
  14.9 23.9 %collective-permute-start.9 = (f32[4,256,128]{2,1,0:T(8,128)S(1)}, f32[4,256,128]{2,1,0:T(8,128)S(1)}, u32[]{:S(2)}, u32[]{:S(2)}) collective-permute-start(f32[4,256,128]{2,1,0:T(8,128)S(1)} %add_select_fusion.1), channel_id=1, source_target_pairs={{0,1},{4,5},{32,33},{36,37},{64,65},{68,69},{96,97},{100,101},{9,1... | collective-permute-start | bytes 1572872 | tf_op jit(solution)/shard_map/ppermute | solution.py:269
  24.5 28.6 %collective-permute-start.17 = (f32[128,8,128]{2,1,0:T(8,128)}, f32[128,8,128]{2,1,0:T(8,128)S(1)}, u32[]{:S(2)}, u32[]{:S(2)}) collective-permute-start(f32[128,8,128]{2,1,0:T(8,128)} %collective-permute-done.15), channel_id=1, source_target_pairs={{32,64},{33,65},{34,66},{35,67},{36,68},{37,69},{38,70},{39,71},{4... | collective-permute-start | bytes 1572872 | tf_op jit(solution)/shard_map/ppermute | solution.py:269
  25.2 12.4 %collective-permute-start.7 = (f32[2,128,128]{2,1,0:T(8,128)S(1)}, f32[2,128,128]{2,1,0:T(8,128)S(1)}, u32[]{:S(2)}, u32[]{:S(2)}) collective-permute-start(f32[2,128,128]{2,1,0:T(8,128)S(1)} %add.46), channel_id=1, source_target_pairs={{0,96},{1,97},{2,98},{3,99},{4,100},{5,101},{6,102},{7,103},{8,104... | collective-permute-start | bytes 393224 | tf_op jit(solution)/shard_map/ppermute | solution.py:269
  37.6 3.8 %collective-permute-start.8 = (f32[2,128,128]{2,1,0:T(8,128)S(1)}, f32[2,128,128]{2,1,0:T(8,128)S(1)}, u32[]{:S(2)}, u32[]{:S(2)}) collective-permute-start(f32[2,128,128]{2,1,0:T(8,128)S(1)} %add.48), channel_id=1, source_target_pairs={{0,32},{1,33},{2,34},{3,35},{4,36},{5,37},{6,38},{7,39},{8,40},{9,... | collective-permute-start | bytes 393224 | tf_op jit(solution)/shard_map/ppermute | solution.py:269
  39.0 23.7 %collective-permute-start.14 = (f32[4,256,128]{2,1,0:T(8,128)S(1)}, f32[4,256,128]{2,1,0:T(8,128)S(1)}, u32[]{:S(2)}, u32[]{:S(2)}) collective-permute-start(f32[4,256,128]{2,1,0:T(8,128)S(1)} %add_add_fusion.g_ref), channel_id=1, source_target_pairs={{0,4},{1,5},{2,6},{3,7},{32,36},{33,37},{34,38},{35,39},{64,68},{6... | collective-permute-start | bytes 1572872 | tf_op jit(solution)/shard_map/ppermute | solution.py:269
  39.4 23.3 %collective-permute-start.13 = (f32[4,256,128]{2,1,0:T(8,128)S(1)}, f32[4,256,128]{2,1,0:T(8,128)S(1)}, u32[]{:S(2)}, u32[]{:S(2)}) collective-permute-start(f32[4,256,128]{2,1,0:T(8,128)S(1)} %add_add_fusion.g_ref), channel_id=1, source_target_pairs={{0,8},{1,9},{2,10},{3,11},{32,40},{33,41},{34,42},{35,43},{64,72},... | collective-permute-start | bytes 1572872 | tf_op jit(solution)/shard_map/ppermute | solution.py:269
  39.4 23.3 %collective-permute-start.12 = (f32[4,256,128]{2,1,0:T(8,128)S(1)}, f32[4,256,128]{2,1,0:T(8,128)S(1)}, u32[]{:S(2)}, u32[]{:S(2)}) collective-permute-start(f32[4,256,128]{2,1,0:T(8,128)S(1)} %add_add_fusion.g_ref), channel_id=1, source_target_pairs={{0,12},{1,13},{2,14},{3,15},{32,44},{33,45},{34,46},{35,47},{64,76... | collective-permute-start | bytes 1572872 | tf_op jit(solution)/shard_map/ppermute | solution.py:269
  41.3 13.0 %collective-permute-start.11 = (f32[2,128,128]{2,1,0:T(8,128)S(1)}, f32[2,128,128]{2,1,0:T(8,128)S(1)}, u32[]{:S(2)}, u32[]{:S(2)}) collective-permute-start(f32[2,128,128]{2,1,0:T(8,128)S(1)} %add.49.mine_ref), channel_id=1, source_target_pairs={{0,16},{1,17},{2,18},{3,19},{4,20},{5,21},{6,22},{7,23},{8,24},{9,... | collective-permute-start | bytes 393224 | tf_op jit(solution)/shard_map/ppermute | solution.py:269
  54.3 8.3 %collective-permute-start.18 = (f32[128,8,128]{2,1,0:T(8,128)S(1)}, f32[128,8,128]{2,1,0:T(8,128)S(1)}, u32[]{:S(2)}, u32[]{:S(2)}) collective-permute-start(f32[128,8,128]{2,1,0:T(8,128)S(1)} %add_select_fusion), channel_id=1, source_target_pairs={{0,16},{1,17},{2,18},{3,19},{4,20},{5,21},{6,22},{7,23},{8,24},{9,... | collective-permute-start | bytes 1572872 | tf_op jit(solution)/shard_map/ppermute | solution.py:269

commit v3 on v2

--- a/solution.py
+++ b/solution.py
@@ -18,7 +18,20 @@
     return high, (x - high.astype(F32)).astype(BF16)
 
 
-def factor_kernel(where_ref, mine_ref, other_ref, lower_ref, inverse_ref, s_ref):
+def gram(a, b):
+    def split3(x):
+        h = x.astype(BF16).astype(F32)
+        mid = (x - h).astype(BF16).astype(F32)
+        return h, mid, x - h - mid
+
+    ah, am, al = split3(a)
+    bh, bm, bl = split3(b)
+    lhs = jnp.concatenate([ah, ah, am, ah, al, am], axis=0).astype(BF16)
+    rhs = jnp.concatenate([bh, bm, bh, bl, bh, bm], axis=0).astype(BF16)
+    return lax.dot_general(lhs, rhs, (((0,), (0,)), ((), ())), preferred_element_type=F32)
+
+
+def factor_kernel(where_ref, mine_ref, other_ref, lower_ref, inverse_ref, whole_ref, s_ref):
     core = where_ref[0]
     size, sub_rows, group = W2, 8, 32
 
@@ -95,28 +108,24 @@
             lo2 = ((o + group) // NB) * NB
             uu = s_ref[o : o + group, lo2 : lo + width]
             left = size - lo2
-            h = uu.astype(BF16).astype(F32)
-            rest = uu - h
-            mid = rest.astype(BF16).astype(F32)
-            low = rest - mid
-            lhs = jnp.concatenate([h, h, mid, h, low, mid], axis=0)[:, :left].astype(BF16)
-            rhs = jnp.concatenate([h, mid, h, low, h, mid], axis=0).astype(BF16)
-            update = lax.dot_general(lhs, rhs, (((0,), (0,)), ((), ())), preferred_element_type=F32)
+            update = gram(uu[:, :left], uu)
             skip = o + group - lo2
             s_ref[o + group : size, lo2 : lo + width] = (
                 s_ref[o + group : size, lo2 : lo + width] - update[skip:, :]
             )
     lower_ref[...] = jnp.where(cols >= rows, s_ref[:, 0:size], 0.0).T
-    inverse_ref[...] = jnp.where(cols <= rows, s_ref[:, size:], 0.0)
+    inverse = jnp.where(cols <= rows, s_ref[:, size:], 0.0)
+    inverse_ref[...] = inverse.T
+    whole_ref[...] = gram(inverse, inverse)
 
 
 def factor_corner(place, mine, other):
     vmem = pl.BlockSpec(memory_space=pltpu.VMEM)
     return pl.pallas_call(
         factor_kernel,
-        out_shape=(jax.ShapeDtypeStruct((W2, W2), F32),) * 2,
+        out_shape=(jax.ShapeDtypeStruct((W2, W2), F32),) * 3,
         in_specs=[pl.BlockSpec(memory_space=pltpu.SMEM), vmem, vmem],
-        out_specs=(vmem, vmem),
+        out_specs=(vmem, vmem, vmem),
         scratch_shapes=[pltpu.VMEM((W2, 2 * W2), F32)],
         compiler_params=pltpu.CompilerParams(vmem_limit_bytes=8 * 1024 * 1024),
         cost_estimate=pl.CostEstimate(flops=8_000_000_000, bytes_accessed=1_000_000, transcendentals=256),
@@ -124,11 +133,11 @@
     )(place, mine, other)
 
 
-STEPS = 8
+STEPS = 4
 
 
 def trailing_kernel(
-    place_ref, lower_ref, inverse_ref, g_ref, gm_ref, gf_ref, gp_ref, columns_ref, m_ref,
+    place_ref, lower_ref, inverse_ref, whole_ref, g_ref, gm_ref, gf_ref, gp_ref, columns_ref, m_ref,
     o_ref, a_ref, old_ref, new_ref, wc_ref, a_sems, m_sems, o_sems,
 ):
     row, col, core, z, y = (place_ref[n] for n in range(5))
@@ -141,17 +150,14 @@
         piece.start()
     loads = [
         pltpu.make_async_copy(
-            m_ref.at[s * TR : (s + 1) * TR], old_ref.at[s], m_sems.at[s]
+            m_ref.at[2 * s * TR : 2 * (s + 1) * TR], old_ref.at[s], m_sems.at[s]
         )
         for s in range(STEPS)
     ]
     for load in loads:
         load.start()
 
-    inverse = inverse_ref[...]
-    high, low = split2(inverse.T)
-    lt = jnp.concatenate([high, low, high], axis=0)
-    high, low = split2(inverse)
+    high, low = split2(whole_ref[...])
     lhs = jnp.concatenate([high, high, low], axis=1)
     for j in range(0, 8, 2):
         x = jnp.concatenate(
@@ -168,29 +174,35 @@
         wc_ref[0:W2, span] = wh
         wc_ref[W2 : 2 * W2, span] = wl
         wc_ref[2 * W2 : 3 * W2, span] = wh
+    for k in range(2):
+
+        @pl.when(col == k)
+        def _():
+            wh, wl = split2(-inverse_ref[:, k * NB : (k + 1) * NB])
+            wc_ref[0:W2, 0:NB] = wh
+            wc_ref[W2 : 2 * W2, 0:NB] = wl
+            wc_ref[2 * W2 : 3 * W2, 0:NB] = wh
+
     for piece in pieces:
         piece.wait()
 
     stores = []
     for s in range(STEPS):
-        half = s // 4
+        half = s // 2
         slot0 = (jnp.where(core == 0, half, 3 * half) - here + 4) % 4
         slot1 = (jnp.where(core == 0, 2 + half, 1 + half) - here + 4) % 4
-        a = jnp.concatenate([a_ref[slot0, s % 4], a_ref[slot1, s % 4]], axis=1)
+        i = 2 * (s % 2)
+        a = jnp.concatenate(
+            [a_ref[slot0, i : i + 2].reshape(2 * TR, NB), a_ref[slot1, i : i + 2].reshape(2 * TR, NB)], axis=1
+        )
         ah, al = split2(a)
-        w = jnp.dot(jnp.concatenate([ah, ah, al], axis=1), lt, preferred_element_type=F32)
-        wh, wl = split2(w)
-        u = jnp.dot(jnp.concatenate([wh, wh, wl], axis=1), wc_ref[...], preferred_element_type=F32)
+        u = jnp.dot(jnp.concatenate([ah, ah, al], axis=1), wc_ref[...], preferred_element_type=F32)
         loads[s].wait()
-        new_ref[s] = old_ref[s] - u.reshape(TR, 8, NB)
-
-        @pl.when(col == 0)
+        new_ref[s] = old_ref[s] - u.reshape(2 * TR, 8, NB)
+
+        @pl.when(col < 2)
         def _():
-            new_ref[s, :, 0, :] = w[:, 0:NB]
-
-        @pl.when(col == 1)
-        def _():
-            new_ref[s, :, 0, :] = w[:, NB:W2]
+            new_ref[s, :, 0, :] = -u[:, 0:NB]
 
         if s == 0:
 
@@ -205,7 +217,7 @@
                     ]
 
         store = pltpu.make_async_copy(
-            new_ref.at[s], o_ref.at[s * TR : (s + 1) * TR], o_sems.at[s]
+            new_ref.at[s], o_ref.at[2 * s * TR : 2 * (s + 1) * TR], o_sems.at[s]
         )
         store.start()
         stores.append(store)
@@ -213,18 +225,18 @@
         store.wait()
 
 
-def update_trailing(place, lower, inverse, pieces, columns, m):
+def update_trailing(place, lower, inverse, whole, pieces, columns, m):
     anywhere = pl.BlockSpec(memory_space=pl.ANY)
     vmem = pl.BlockSpec(memory_space=pltpu.VMEM)
     return pl.pallas_call(
         trailing_kernel,
         out_shape=jax.ShapeDtypeStruct(m.shape, F32),
-        in_specs=[pl.BlockSpec(memory_space=pltpu.SMEM), vmem, vmem] + [anywhere] * 4 + [vmem, anywhere],
+        in_specs=[pl.BlockSpec(memory_space=pltpu.SMEM), vmem, vmem, vmem] + [anywhere] * 4 + [vmem, anywhere],
         out_specs=anywhere,
         scratch_shapes=[
             pltpu.VMEM((4, 4, TR, NB), F32),
-            pltpu.VMEM((STEPS, TR, 8, NB), F32),
-            pltpu.VMEM((STEPS, TR, 8, NB), F32),
+            pltpu.VMEM((STEPS, 2 * TR, 8, NB), F32),
+            pltpu.VMEM((STEPS, 2 * TR, 8, NB), F32),
             pltpu.VMEM((3 * W2, 8 * NB), BF16),
             pltpu.SemaphoreType.DMA((4,)),
             pltpu.SemaphoreType.DMA((STEPS,)),
@@ -233,7 +245,7 @@
         compiler_params=pltpu.CompilerParams(vmem_limit_bytes=36 * 1024 * 1024),
         cost_estimate=pl.CostEstimate(flops=4_000_000_000, bytes_accessed=20_000_000, transcendentals=0),
         name="trailing_update",
-    )(place, lower, inverse, *pieces, columns, m)
+    )(place, lower, inverse, whole, *pieces, columns, m)
 
 
 def device(x, core, z, y):
@@ -379,10 +391,10 @@
     g1, g3, g2 = (send(g, moves) for moves in around)
     c = jnp.where(x == 0, top, c1 + c2 + c3)
     c = after(c, other)
-    lower, inverse = factor_corner(place[2:3], mine, other)
+    lower, inverse, whole = factor_corner(place[2:3], mine, other)
     columns = jnp.stack([c, send(c, SWAP)])
     columns = jnp.where(core == 0, columns, columns[::-1])
-    result = update_trailing(place, lower, inverse, (g, g3, g2, g1), columns, m)
+    result = update_trailing(place, lower, inverse, whole, (g, g3, g2, g1), columns, m)
     return result.reshape(kernel.shape)
 
 

time: 75.6 us -> 73.7 us (0.975)
  Pallas kernels: 22.3 us -> 20.4 us
    pallas_call x1, Pallas kernels: 12.2 us -> 9.92 us  [update_trailing(): pl.pallas_call(trailing_kernel, out_shape=jax.ShapeDtypeStruct(m.shape, F...]
  transfers between devices with their start and end apart: 19 -> 19, of which waited for: 3 -> 3; matrix products, arithmetic and copies ran while one was open for 2% -> 2% of each run, Pallas kernels for 11% -> 12%
where the time goes in v3:
time: 73.7 us; the launch traced here: 73.3 us
  starting transfers between devices  30.2 us (41%)
  waiting for transfers between devices  20.5 us (28%)
  Pallas kernels  20.4 us (28%)
  other arithmetic  1.67 us (2%)
    ppermute x19, starting transfers between devices, send(): return lax.ppermute(value, BOTH, moves)  30.2 us
    ppermute x19, waiting for transfers between devices, send(): return lax.ppermute(value, BOTH, moves)  20.5 us
    pallas_call x1, Pallas kernels, update_trailing(): pl.pallas_call(trailing_kernel, out_shape=jax.ShapeDtypeStruct(m.shape, F...  9.92 us
    pallas_call x1, Pallas kernels, factor_corner(): pl.pallas_call(factor_kernel, out_shape=(jax.ShapeDtypeStruct((W2, W2), F...  8.56 us
    pallas_call x1, Pallas kernels, extract(): pl.pallas_call(extract_kernel, out_shape=(half, half, jax.ShapeDtypeStruc...  1.92 us
  transfers between devices with their start and end apart: 19, of which 3 were waited for; matrix products, arithmetic and copies ran while one was open for 2% of the time, Pallas kernels for 12%

profile of v3, /device:TPU:15, one launch (start us, length us, event | category | flops | bytes accessed | tf_op | source)
XLA Modules:
  0.0 73.3 jit_solution(11951316326284667305)
XLA Ops:
  0.1 1.9 %extract_panels.1 = (f32[4,256,128]{2,1,0:T(8,128)S(1)}, f32[4,256,128]{2,1,0:T(8,128)S(1)}, f32[128,128]{1,0:T(8,128)S(1)}, f32[128,8,128]{2,1,0:T(8,128)S(1)}) custom-call(s32[6]{0:T(128)S(1)} %stack.50.place_ref, f32[2048,8,128]{2,1,0:T(8,128)} %bitcast.17), custom_call_target="tpu_custom_call" | custom-call | bytes 4000000 | tf_op jit(solution)/shard_map/extract_panels/pallas_call | solution.py:330
  2.0 0.7 collective-permute-start
  2.7 0.7 collective-permute-start.1
  3.4 2.0 %collective-permute-start.4 = (f32[4,256,128]{2,1,0:T(8,128)S(1)}, f32[4,256,128]{2,1,0:T(8,128)S(1)}, u32[]{:S(2)}, u32[]{:S(2)}) collective-permute-start(f32[4,256,128]{2,1,0:T(8,128)S(1)} %get-tuple-element.19), channel_id=1, source_target_pairs={{0,4},{32,36},{64,68},{96,100},{1,13},{33,45},{65,77},{97,109},{16... | collective-permute-start | bytes 1572872 | tf_op jit(solution)/shard_map/ppermute | solution.py:281
  5.4 0.7 collective-permute-start.5
  6.1 0.7 collective-permute-start.2
  6.9 0.7 collective-permute-start.3
  7.5 1.3 %collective-permute-start.16 = (f32[128,8,128]{2,1,0:T(8,128)S(1)}, f32[128,8,128]{2,1,0:T(8,128)S(1)}, u32[]{:S(2)}, u32[]{:S(2)}) collective-permute-start(f32[128,8,128]{2,1,0:T(8,128)S(1)} %get-tuple-element.26), channel_id=1, source_target_pairs={{0,96},{1,97},{2,98},{3,99},{4,100},{5,101},{6,102},{7,103},{8,104... | collective-permute-start | bytes 1572872 | tf_op jit(solution)/shard_map/ppermute | solution.py:281
  8.8 1.5 %collective-permute-start.15 = (f32[128,8,128]{2,1,0:T(8,128)S(1)}, f32[128,8,128]{2,1,0:T(8,128)}, u32[]{:S(2)}, u32[]{:S(2)}) collective-permute-start(f32[128,8,128]{2,1,0:T(8,128)S(1)} %get-tuple-element.26), channel_id=1, source_target_pairs={{0,32},{1,33},{2,34},{3,35},{4,36},{5,37},{6,38},{7,39},{8,40},{9,... | collective-permute-start | bytes 1572872 | tf_op jit(solution)/shard_map/ppermute | solution.py:281
  10.3 1.2 %collective-permute-done.4 = f32[4,256,128]{2,1,0:T(8,128)S(1)} collective-permute-done((f32[4,256,128]{2,1,0:T(8,128)S(1)}, f32[4,256,128]{2,1,0:T(8,128)S(1)}, u32[]{:S(2)}, u32[]{:S(2)}) %collective-permute-start.4) | collective-permute-done | bytes 524320 | tf_op jit(solution)/shard_map/ppermute | solution.py:281
  11.6 2.0 %collective-permute-start.6 = (f32[4,256,128]{2,1,0:T(8,128)S(1)}, f32[4,256,128]{2,1,0:T(8,128)S(1)}, u32[]{:S(2)}, u32[]{:S(2)}) collective-permute-start(f32[4,256,128]{2,1,0:T(8,128)S(1)} %add_select_fusion.1), channel_id=1, source_target_pairs={{0,3},{4,7},{32,35},{36,39},{64,67},{68,71},{96,99},{100,103},{9,8... | collective-permute-start | bytes 1572872 | tf_op jit(solution)/shard_map/ppermute | solution.py:281
  13.6 1.3 %collective-permute-start.10 = (f32[4,256,128]{2,1,0:T(8,128)S(1)}, f32[4,256,128]{2,1,0:T(8,128)S(1)}, u32[]{:S(2)}, u32[]{:S(2)}) collective-permute-start(f32[4,256,128]{2,1,0:T(8,128)S(1)} %add_select_fusion.1), channel_id=1, source_target_pairs={{0,2},{4,6},{32,34},{36,38},{64,66},{68,70},{96,98},{100,102},{9,1... | collective-permute-start | bytes 1572872 | tf_op jit(solution)/shard_map/ppermute | solution.py:281
  14.9 1.3 %collective-permute-start.9 = (f32[4,256,128]{2,1,0:T(8,128)S(1)}, f32[4,256,128]{2,1,0:T(8,128)S(1)}, u32[]{:S(2)}, u32[]{:S(2)}) collective-permute-start(f32[4,256,128]{2,1,0:T(8,128)S(1)} %add_select_fusion.1), channel_id=1, source_target_pairs={{0,1},{4,5},{32,33},{36,37},{64,65},{68,69},{96,97},{100,101},{9,1... | collective-permute-start | bytes 1572872 | tf_op jit(solution)/shard_map/ppermute | solution.py:281
  16.3 8.2 %collective-permute-done.16 = f32[128,8,128]{2,1,0:T(8,128)S(1)} collective-permute-done((f32[128,8,128]{2,1,0:T(8,128)S(1)}, f32[128,8,128]{2,1,0:T(8,128)S(1)}, u32[]{:S(2)}, u32[]{:S(2)}) %collective-permute-start.16) | collective-permute-done | bytes 524320 | tf_op jit(solution)/shard_map/ppermute | solution.py:281
  24.5 0.7 collective-permute-start.17
  25.2 1.3 %collective-permute-start.7 = (f32[2,128,128]{2,1,0:T(8,128)S(1)}, f32[2,128,128]{2,1,0:T(8,128)S(1)}, u32[]{:S(2)}, u32[]{:S(2)}) collective-permute-start(f32[2,128,128]{2,1,0:T(8,128)S(1)} %add.46), channel_id=1, source_target_pairs={{0,96},{1,97},{2,98},{3,99},{4,100},{5,101},{6,102},{7,103},{8,104... | collective-permute-start | bytes 393224 | tf_op jit(solution)/shard_map/ppermute | solution.py:281
  26.5 11.1 %collective-permute-done.7 = f32[2,128,128]{2,1,0:T(8,128)S(1)} collective-permute-done((f32[2,128,128]{2,1,0:T(8,128)S(1)}, f32[2,128,128]{2,1,0:T(8,128)S(1)}, u32[]{:S(2)}, u32[]{:S(2)}) %collective-permute-start.7) | collective-permute-done | bytes 131104 | tf_op jit(solution)/shard_map/ppermute | solution.py:281
  37.6 1.3 %collective-permute-start.8 = (f32[2,128,128]{2,1,0:T(8,128)S(1)}, f32[2,128,128]{2,1,0:T(8,128)S(1)}, u32[]{:S(2)}, u32[]{:S(2)}) collective-permute-start(f32[2,128,128]{2,1,0:T(8,128)S(1)} %add.48), channel_id=1, source_target_pairs={{0,32},{1,33},{2,34},{3,35},{4,36},{5,37},{6,38},{7,39},{8,40},{9,... | collective-permute-start | bytes 393224 | tf_op jit(solution)/shard_map/ppermute | solution.py:281
  39.0 0.4 collective-permute-start.14
  39.4 1.9 %collective-permute-start.12 = (f32[4,256,128]{2,1,0:T(8,128)S(1)}, f32[4,256,128]{2,1,0:T(8,128)S(1)}, u32[]{:S(2)}, u32[]{:S(2)}) collective-permute-start(f32[4,256,128]{2,1,0:T(8,128)S(1)} %add_add_fusion.g_ref), channel_id=1, source_target_pairs={{0,12},{1,13},{2,14},{3,15},{32,44},{33,45},{34,46},{35,47},{64,76... | collective-permute-start | bytes 1572872 | tf_op jit(solution)/shard_map/ppermute | solution.py:281
  41.3 11.8 %collective-permute-start.11 = (f32[2,128,128]{2,1,0:T(8,128)S(1)}, f32[2,128,128]{2,1,0:T(8,128)S(1)}, u32[]{:S(2)}, u32[]{:S(2)}) collective-permute-start(f32[2,128,128]{2,1,0:T(8,128)S(1)} %add.49.mine_ref), channel_id=1, source_target_pairs={{0,16},{1,17},{2,18},{3,19},{4,20},{5,21},{6,22},{7,23},{8,24},{9,... | collective-permute-start | bytes 393224 | tf_op jit(solution)/shard_map/ppermute | solution.py:281
  53.1 1.2 %add_select_fusion = f32[128,8,128]{2,1,0:T(8,128)S(1)} fusion(f32[128,8,128]{2,1,0:T(8,128)S(1)} %get-tuple-element.26, f32[128,8,128]{2,1,0:T(8,128)S(1)} %collective-permute-done.16, f32[128,8,128]{2,1,0:T(8,128)} %collective-permute-done.15, f32[128,8,128]{2,1,0:T(8,128)S(1)} %collective-permute-done.17, pred[]{:T(512)S(6)} %eq.19), kind=kLoop, calls=%fused_computation.2 | loop fusion | flops 393216 | bytes 2621441 | tf_op jit(solution)/shard_map/jit(_where)/select_n | solution.py:392
  54.5 8.6 %corner_factor.1 = (f32[256,256]{1,0:T(8,128)S(1)}, f32[256,256]{1,0:T(8,128)S(1)}, f32[256,256]{1,0:T(8,128)S(1)}) custom-call(s32[1]{0:T(128)} %bitcast.2.where_ref, f32[2,128,128]{2,1,0:T(8,128)S(1)} %add.49.mine_ref, f32[2,128,128]{2,1,0:T(8,128)S(1)} %collective-permute-done.11.other_ref), custom_call_target="tpu_custom_call" | custom-call | flops 8000000000 | bytes 1000000 | tf_op jit(solution)/shard_map/corner_factor/pallas_call | solution.py:124
  63.2 9.9 %trailing_update.1 = f32[2048,8,128]{2,1,0:T(8,128)} custom-call(s32[6]{0:T(128)S(1)} %stack.50.place_ref, f32[256,256]{1,0:T(8,128)S(1)} %get-tuple-element.23.lower_ref, f32[256,256]{1,0:T(8,128)S(1)} %get-tuple-element.24.inverse_ref, f32[256,256]{1,0:T(8,128)S(1)} %get-tuple-element.25.whole_ref, f32[4,256,128]{2,1,0:T(8,128)S(1)} %add_add_fusion.g_ref, ...), custom_call_target="tpu_custom_call" | custom-call | flops 4000000000 | bytes 20000000 | tf_op jit(solution)/shard_map/trailing_update/pallas_call | solution.py:231
  (29 shorter events, 0.7 us)
Async XLA Ops:
  2.0 0.7 collective-permute-start
  2.7 3.4 %collective-permute-start.1 = (f32[2,128,128]{2,1,0:T(8,128)S(1)}, f32[2,128,128]{2,1,0:T(8,128)S(1)}, u32[]{:S(2)}, u32[]{:S(2)}) collective-permute-start(f32[2,128,128]{2,1,0:T(8,128)S(1)} %fusion), channel_id=1, source_target_pairs={{0,4},{1,5},{16,20},{17,21}} | collective-permute-start | bytes 393224 | tf_op jit(solution)/shard_map/ppermute | solution.py:281
  3.4 8.1 %collective-permute-start.4 = (f32[4,256,128]{2,1,0:T(8,128)S(1)}, f32[4,256,128]{2,1,0:T(8,128)S(1)}, u32[]{:S(2)}, u32[]{:S(2)}) collective-permute-start(f32[4,256,128]{2,1,0:T(8,128)S(1)} %get-tuple-element.19), channel_id=1, source_target_pairs={{0,4},{32,36},{64,68},{96,100},{1,13},{33,45},{65,77},{97,109},{16... | collective-permute-start | bytes 1572872 | tf_op jit(solution)/shard_map/ppermute | solution.py:281
  5.4 6.1 %collective-permute-start.5 = (f32[4,256,128]{2,1,0:T(8,128)S(1)}, f32[4,256,128]{2,1,0:T(8,128)S(1)}, u32[]{:S(2)}, u32[]{:S(2)}) collective-permute-start(f32[4,256,128]{2,1,0:T(8,128)S(1)} %get-tuple-element.18), channel_id=1, source_target_pairs={{1,9},{33,41},{65,73},{97,105}} | collective-permute-start | bytes 1572872 | tf_op jit(solution)/shard_map/ppermute | solution.py:281
  6.1 0.7 collective-permute-start.2
  6.9 3.4 %collective-permute-start.3 = (f32[2,128,128]{2,1,0:T(8,128)S(1)}, f32[2,128,128]{2,1,0:T(8,128)S(1)}, u32[]{:S(2)}, u32[]{:S(2)}) collective-permute-start(f32[2,128,128]{2,1,0:T(8,128)S(1)} %fusion.2), channel_id=1, source_target_pairs={{0,3},{4,7},{8,11},{12,15},{16,19},{20,23},{24,27},{28,31},{1,2},{... | collective-permute-start | bytes 393224 | tf_op jit(solution)/shard_map/ppermute | solution.py:281
  7.5 16.9 %collective-permute-start.16 = (f32[128,8,128]{2,1,0:T(8,128)S(1)}, f32[128,8,128]{2,1,0:T(8,128)S(1)}, u32[]{:S(2)}, u32[]{:S(2)}) collective-permute-start(f32[128,8,128]{2,1,0:T(8,128)S(1)} %get-tuple-element.26), channel_id=1, source_target_pairs={{0,96},{1,97},{2,98},{3,99},{4,100},{5,101},{6,102},{7,103},{8,104... | collective-permute-start | bytes 1572872 | tf_op jit(solution)/shard_map/ppermute | solution.py:281
  8.8 15.6 %collective-permute-start.15 = (f32[128,8,128]{2,1,0:T(8,128)S(1)}, f32[128,8,128]{2,1,0:T(8,128)}, u32[]{:S(2)}, u32[]{:S(2)}) collective-permute-start(f32[128,8,128]{2,1,0:T(8,128)S(1)} %get-tuple-element.26), channel_id=1, source_target_pairs={{0,32},{1,33},{2,34},{3,35},{4,36},{5,37},{6,38},{7,39},{8,40},{9,... | collective-permute-start | bytes 1572872 | tf_op jit(solution)/shard_map/ppermute | solution.py:281
  11.6 13.6 %collective-permute-start.6 = (f32[4,256,128]{2,1,0:T(8,128)S(1)}, f32[4,256,128]{2,1,0:T(8,128)S(1)}, u32[]{:S(2)}, u32[]{:S(2)}) collective-permute-start(f32[4,256,128]{2,1,0:T(8,128)S(1)} %add_select_fusion.1), channel_id=1, source_target_pairs={{0,3},{4,7},{32,35},{36,39},{64,67},{68,71},{96,99},{100,103},{9,8... | collective-permute-start | bytes 1572872 | tf_op jit(solution)/shard_map/ppermute | solution.py:281
  13.6 25.3 %collective-permute-start.10 = (f32[4,256,128]{2,1,0:T(8,128)S(1)}, f32[4,256,128]{2,1,0:T(8,128)S(1)}, u32[]{:S(2)}, u32[]{:S(2)}) collective-permute-start(f32[4,256,128]{2,1,0:T(8,128)S(1)} %add_select_fusion.1), channel_id=1, source_target_pairs={{0,2},{4,6},{32,34},{36,38},{64,66},{68,70},{96,98},{100,102},{9,1... | collective-permute-start | bytes 1572872 | tf_op jit(solution)/shard_map/ppermute | solution.py:281
  14.9 23.9 %collective-permute-start.9 = (f32[4,256,128]{2,1,0:T(8,128)S(1)}, f32[4,256,128]{2,1,0:T(8,128)S(1)}, u32[]{:S(2)}, u32[]{:S(2)}) collective-permute-start(f32[4,256,128]{2,1,0:T(8,128)S(1)} %add_select_fusion.1), channel_id=1, source_target_pairs={{0,1},{4,5},{32,33},{36,37},{64,65},{68,69},{96,97},{100,101},{9,1... | collective-permute-start | bytes 1572872 | tf_op jit(solution)/shard_map/ppermute | solution.py:281
  24.5 28.6 %collective-permute-start.17 = (f32[128,8,128]{2,1,0:T(8,128)}, f32[128,8,128]{2,1,0:T(8,128)S(1)}, u32[]{:S(2)}, u32[]{:S(2)}) collective-permute-start(f32[128,8,128]{2,1,0:T(8,128)} %collective-permute-done.15), channel_id=1, source_target_pairs={{32,64},{33,65},{34,66},{35,67},{36,68},{37,69},{38,70},{39,71},{4... | collective-permute-start | bytes 1572872 | tf_op jit(solution)/shard_map/ppermute | solution.py:281
  25.2 12.4 %collective-permute-start.7 = (f32[2,128,128]{2,1,0:T(8,128)S(1)}, f32[2,128,128]{2,1,0:T(8,128)S(1)}, u32[]{:S(2)}, u32[]{:S(2)}) collective-permute-start(f32[2,128,128]{2,1,0:T(8,128)S(1)} %add.46), channel_id=1, source_target_pairs={{0,96},{1,97},{2,98},{3,99},{4,100},{5,101},{6,102},{7,103},{8,104... | collective-permute-start | bytes 393224 | tf_op jit(solution)/shard_map/ppermute | solution.py:281
  37.6 3.8 %collective-permute-start.8 = (f32[2,128,128]{2,1,0:T(8,128)S(1)}, f32[2,128,128]{2,1,0:T(8,128)S(1)}, u32[]{:S(2)}, u32[]{:S(2)}) collective-permute-start(f32[2,128,128]{2,1,0:T(8,128)S(1)} %add.48), channel_id=1, source_target_pairs={{0,32},{1,33},{2,34},{3,35},{4,36},{5,37},{6,38},{7,39},{8,40},{9,... | collective-permute-start | bytes 393224 | tf_op jit(solution)/shard_map/ppermute | solution.py:281
  39.0 24.2 %collective-permute-start.14 = (f32[4,256,128]{2,1,0:T(8,128)S(1)}, f32[4,256,128]{2,1,0:T(8,128)S(1)}, u32[]{:S(2)}, u32[]{:S(2)}) collective-permute-start(f32[4,256,128]{2,1,0:T(8,128)S(1)} %add_add_fusion.g_ref), channel_id=1, source_target_pairs={{0,4},{1,5},{2,6},{3,7},{32,36},{33,37},{34,38},{35,39},{64,68},{6... | collective-permute-start | bytes 1572872 | tf_op jit(solution)/shard_map/ppermute | solution.py:281
  39.4 23.8 %collective-permute-start.13 = (f32[4,256,128]{2,1,0:T(8,128)S(1)}, f32[4,256,128]{2,1,0:T(8,128)S(1)}, u32[]{:S(2)}, u32[]{:S(2)}) collective-permute-start(f32[4,256,128]{2,1,0:T(8,128)S(1)} %add_add_fusion.g_ref), channel_id=1, source_target_pairs={{0,8},{1,9},{2,10},{3,11},{32,40},{33,41},{34,42},{35,43},{64,72},... | collective-permute-start | bytes 1572872 | tf_op jit(solution)/shard_map/ppermute | solution.py:281
  39.4 23.8 %collective-permute-start.12 = (f32[4,256,128]{2,1,0:T(8,128)S(1)}, f32[4,256,128]{2,1,0:T(8,128)S(1)}, u32[]{:S(2)}, u32[]{:S(2)}) collective-permute-start(f32[4,256,128]{2,1,0:T(8,128)S(1)} %add_add_fusion.g_ref), channel_id=1, source_target_pairs={{0,12},{1,13},{2,14},{3,15},{32,44},{33,45},{34,46},{35,47},{64,76... | collective-permute-start | bytes 1572872 | tf_op jit(solution)/shard_map/ppermute | solution.py:281
  41.3 13.0 %collective-permute-start.11 = (f32[2,128,128]{2,1,0:T(8,128)S(1)}, f32[2,128,128]{2,1,0:T(8,128)S(1)}, u32[]{:S(2)}, u32[]{:S(2)}) collective-permute-start(f32[2,128,128]{2,1,0:T(8,128)S(1)} %add.49.mine_ref), channel_id=1, source_target_pairs={{0,16},{1,17},{2,18},{3,19},{4,20},{5,21},{6,22},{7,23},{8,24},{9,... | collective-permute-start | bytes 393224 | tf_op jit(solution)/shard_map/ppermute | solution.py:281
  54.3 8.7 %collective-permute-start.18 = (f32[128,8,128]{2,1,0:T(8,128)S(1)}, f32[128,8,128]{2,1,0:T(8,128)S(1)}, u32[]{:S(2)}, u32[]{:S(2)}) collective-permute-start(f32[128,8,128]{2,1,0:T(8,128)S(1)} %add_select_fusion), channel_id=1, source_target_pairs={{0,16},{1,17},{2,18},{3,19},{4,20},{5,21},{6,22},{7,23},{8,24},{9,... | collective-permute-start | bytes 1572872 | tf_op jit(solution)/shard_map/ppermute | solution.py:281

commit v4 on v3

--- a/solution.py
+++ b/solution.py
@@ -133,7 +133,7 @@
     )(place, mine, other)
 
 
-STEPS = 4
+STEPS = ((0, 2), (2, 4), (4, 6), (6, 7), (7, 8))
 
 
 def trailing_kernel(
@@ -149,10 +149,8 @@
     for piece in pieces:
         piece.start()
     loads = [
-        pltpu.make_async_copy(
-            m_ref.at[2 * s * TR : 2 * (s + 1) * TR], old_ref.at[s], m_sems.at[s]
-        )
-        for s in range(STEPS)
+        pltpu.make_async_copy(m_ref.at[i * TR : j * TR], old_ref.at[i * TR : j * TR], m_sems.at[n])
+        for n, (i, j) in enumerate(STEPS)
     ]
     for load in loads:
         load.start()
@@ -187,38 +185,38 @@
         piece.wait()
 
     stores = []
-    for s in range(STEPS):
-        half = s // 2
+    for n, (first, last) in enumerate(STEPS):
+        half = first // 4
         slot0 = (jnp.where(core == 0, half, 3 * half) - here + 4) % 4
         slot1 = (jnp.where(core == 0, 2 + half, 1 + half) - here + 4) % 4
-        i = 2 * (s % 2)
+        span = pl.ds(first % 4, last - first)
+        count = (last - first) * TR
         a = jnp.concatenate(
-            [a_ref[slot0, i : i + 2].reshape(2 * TR, NB), a_ref[slot1, i : i + 2].reshape(2 * TR, NB)], axis=1
+            [a_ref[slot0, span].reshape(count, NB), a_ref[slot1, span].reshape(count, NB)], axis=1
         )
         ah, al = split2(a)
         u = jnp.dot(jnp.concatenate([ah, ah, al], axis=1), wc_ref[...], preferred_element_type=F32)
-        loads[s].wait()
-        new_ref[s] = old_ref[s] - u.reshape(2 * TR, 8, NB)
+        loads[n].wait()
+        span = pl.ds(first * TR, count)
+        new_ref[span] = old_ref[span] - u.reshape(count, 8, NB)
 
         @pl.when(col < 2)
         def _():
-            new_ref[s, :, 0, :] = -u[:, 0:NB]
-
-        if s == 0:
+            new_ref[span, 0, :] = -u[:, 0:NB]
+
+        if n == 0:
 
             @pl.when(row < 2)
             def _():
-                new_ref[s, 0:NB, :, :] = jnp.zeros((NB, 8, NB), F32)
+                new_ref[0:NB, :, :] = jnp.zeros((NB, 8, NB), F32)
 
                 @pl.when(col < 2)
                 def _():
-                    new_ref[s, 0:NB, 0, :] = lower_ref[
+                    new_ref[0:NB, 0, :] = lower_ref[
                         pl.ds(pl.multiple_of(row * NB, NB), NB), pl.ds(pl.multiple_of(col * NB, NB), NB)
                     ]
 
-        store = pltpu.make_async_copy(
-            new_ref.at[s], o_ref.at[2 * s * TR : 2 * (s + 1) * TR], o_sems.at[s]
-        )
+        store = pltpu.make_async_copy(new_ref.at[span], o_ref.at[span], o_sems.at[n])
         store.start()
         stores.append(store)
     for store in stores:
@@ -235,12 +233,12 @@
         out_specs=anywhere,
         scratch_shapes=[
             pltpu.VMEM((4, 4, TR, NB), F32),
-            pltpu.VMEM((STEPS, 2 * TR, 8, NB), F32),
-            pltpu.VMEM((STEPS, 2 * TR, 8, NB), F32),
+            pltpu.VMEM(m.shape, F32),
+            pltpu.VMEM(m.shape, F32),
             pltpu.VMEM((3 * W2, 8 * NB), BF16),
             pltpu.SemaphoreType.DMA((4,)),
-            pltpu.SemaphoreType.DMA((STEPS,)),
-            pltpu.SemaphoreType.DMA((STEPS,)),
+            pltpu.SemaphoreType.DMA((len(STEPS),)),
+            pltpu.SemaphoreType.DMA((len(STEPS),)),
         ],
         compiler_params=pltpu.CompilerParams(vmem_limit_bytes=36 * 1024 * 1024),
         cost_estimate=pl.CostEstimate(flops=4_000_000_000, bytes_accessed=20_000_000, transcendentals=0),
@@ -348,23 +346,22 @@
     m = pltpu.with_memory_space_constraint(m, pltpu.HBM)
     first, second, e, top = extract(place, m)
 
-    plane = (0,)
-    f = send(e, pairs(along_y([(0, 1), (1, 0)], xs=plane, zs=(0,))))
-
-    lay_y = along_y([(0, 3), (1, 2)], cores=(1,), zs=(0,))
-    r1 = send(second, pairs(along_z([(0, 1)], (0,), (0,)) + along_z([(0, 3)], (0,), (1,)) + lay_y))
-    r2 = send(first, pairs(along_z([(0, 2)], (0,), (1,))))
-    c1, c3 = (send(top, along_x([(0, to)])) for to in (1, 3))
-
+    f = send(e, pairs(along_y([(0, 1), (1, 0)], xs=(0,), zs=(0,))))
     e = jnp.where(y == 0, jnp.stack([e, f]), jnp.stack([f, e]))
     e = jnp.where((x == 0) & (z == 0) & (y < 2), e, 0.0)
-    e = e + send(e, pairs(along_z([(0, 1)], ys=(0, 1), xs=plane)))
-    e = e + send(e, pairs(along_z([(0, 3), (1, 2)], ys=(0, 1), xs=plane)))
-    e = e + send(e, pairs(along_y([(0, 3), (1, 2)], xs=plane)))
+    x3, x1, x2 = (send(e, along_x([(0, to)])) for to in (3, 1, 2))
+    e = e + x1 + x2 + x3
+
+    lay_y = along_y([(0, 3), (1, 2)], cores=(1,), zs=(0,))
+    near = pairs(along_z([(0, 1)], (0,), (0,)) + along_z([(0, 3)], (0,), (1,)) + lay_y)
+    far = pairs(along_z([(0, 2)], (0,), (1,)))
+    r1, r2 = send(second, near), send(first, far)
+    e1, e2 = send(e, near), send(e, far)
 
     kept = (z == 0) & jnp.where(core == 0, y == 0, y < 2)
-    own = jnp.where(kept, first, r1 + r2)
-    own = after(own, e)
+    own = jnp.concatenate(
+        [jnp.where(kept, first, r1 + r2).reshape(8, NB, NB), jnp.where(kept, e, e1 + e2)]
+    )
     lines = [
         pairs(
             along_y([(0, d % 4)], (0,), (0, 1))
@@ -374,14 +371,15 @@
         for d in (1, 3, 2)
     ]
     b1, b3, b2 = (send(own, moves) for moves in lines)
-    c2 = send(after(c1, c3, e), along_x([(1, 2)]))
-
-    e = after(e, b3)
-    e = e + send(e, along_x([(0, 3)]))
-    mine = e + send(e, along_x([(0, 1), (3, 2)]))
+    top = after(top, own)
+    c1, c3 = (send(top, along_x([(0, to)])) for to in (1, 3))
+    c2 = send(c1, along_x([(1, 2)]))
     g = own + b1 + b2 + b3
-    mine = after(mine, g)
+    e, g = g[8:], g[:8].reshape(4, TR, NB)
+
+    mine = e
     other = send(mine, SWAP)
+    g = after(g, other)
     around = [
         pairs(
             along_z([(a, (a + d) % 4) for a in SPAN], (0,)) + along_y([(a, (a + d) % 4) for a in SPAN], (1,))
@@ -390,7 +388,6 @@
     ]
     g1, g3, g2 = (send(g, moves) for moves in around)
     c = jnp.where(x == 0, top, c1 + c2 + c3)
-    c = after(c, other)
     lower, inverse, whole = factor_corner(place[2:3], mine, other)
     columns = jnp.stack([c, send(c, SWAP)])
     columns = jnp.where(core == 0, columns, columns[::-1])

time: 73.7 us -> 72.3 us (0.981)
  the two profiles are of different devices: /device:TPU:15 before, /device:TPU:88 now
where the time goes in v4:
time: 72.3 us; the launch traced here: 71.9 us
  waiting for transfers between devices  30.2 us (42%)
  starting transfers between devices  21.2 us (29%)
  Pallas kernels  19.2 us (27%)
    ppermute x19, waiting for transfers between devices, send(): return lax.ppermute(value, BOTH, moves)  30.2 us
    ppermute x19, starting transfers between devices, send(): return lax.ppermute(value, BOTH, moves)  21.2 us
    pallas_call x1, Pallas kernels, update_trailing(): pl.pallas_call(trailing_kernel, out_shape=jax.ShapeDtypeStruct(m.shape, F...  8.99 us
    pallas_call x1, Pallas kernels, factor_corner(): pl.pallas_call(factor_kernel, out_shape=(jax.ShapeDtypeStruct((W2, W2), F...  8.56 us
    pallas_call x1, Pallas kernels, extract(): pl.pallas_call(extract_kernel, out_shape=(half, half, jax.ShapeDtypeStruc...  1.68 us
  transfers between devices with their start and end apart: 19, of which 6 were waited for; matrix products, arithmetic and copies ran while one was open for 1% of the time, Pallas kernels for 12%

profile of v4, /device:TPU:88, one launch (start us, length us, event | category | flops | bytes accessed | tf_op | source)
XLA Modules:
  0.0 71.9 jit_solution(13971745679485125482)
XLA Ops:
  0.1 1.7 %extract_panels.1 = (f32[4,256,128]{2,1,0:T(8,128)S(1)}, f32[4,256,128]{2,1,0:T(8,128)S(1)}, f32[128,128]{1,0:T(8,128)S(1)}, f32[128,8,128]{2,1,0:T(8,128)S(1)}) custom-call(s32[6]{0:T(128)S(1)} %stack.50.place_ref, f32[2048,8,128]{2,1,0:T(8,128)} %bitcast.22), custom_call_target="tpu_custom_call" | custom-call | bytes 4000000 | tf_op jit(solution)/shard_map/extract_panels/pallas_call | solution.py:328
  1.8 0.7 collective-permute-start.2
  2.5 3.9 %collective-permute-start.4 = (f32[2,128,128]{2,1,0:T(8,128)S(1)}, f32[2,128,128]{2,1,0:T(8,128)S(1)}, u32[]{:S(2)}, u32[]{:S(2)}) collective-permute-start(f32[2,128,128]{2,1,0:T(8,128)S(1)} %fusion), channel_id=1, source_target_pairs={{0,64},{1,65},{2,66},{3,67},{4,68},{5,69},{6,70},{7,71},{8,72},{9,... | collective-permute-start | bytes 393224 | tf_op jit(solution)/shard_map/ppermute | solution.py:279
  6.4 1.3 %collective-permute-start.5 = (f32[2,128,128]{2,1,0:T(8,128)S(1)}, f32[2,128,128]{2,1,0:T(8,128)S(1)}, u32[]{:S(2)}, u32[]{:S(2)}) collective-permute-start(f32[2,128,128]{2,1,0:T(8,128)S(1)} %fusion), channel_id=1, source_target_pairs={{0,96},{1,97},{2,98},{3,99},{4,100},{5,101},{6,102},{7,103},{8,104... | collective-permute-start | bytes 393224 | tf_op jit(solution)/shard_map/ppermute | solution.py:279
  7.7 1.3 %collective-permute-start.3 = (f32[2,128,128]{2,1,0:T(8,128)S(1)}, f32[2,128,128]{2,1,0:T(8,128)S(1)}, u32[]{:S(2)}, u32[]{:S(2)}) collective-permute-start(f32[2,128,128]{2,1,0:T(8,128)S(1)} %fusion), channel_id=1, source_target_pairs={{0,32},{1,33},{2,34},{3,35},{4,36},{5,37},{6,38},{7,39},{8,40},{9,... | collective-permute-start | bytes 393224 | tf_op jit(solution)/shard_map/ppermute | solution.py:279
  9.0 0.7 collective-permute-start
  9.7 0.7 collective-permute-start.1
  10.5 1.5 %collective-permute-done.3 = f32[2,128,128]{2,1,0:T(8,128)S(1)} collective-permute-done((f32[2,128,128]{2,1,0:T(8,128)S(1)}, f32[2,128,128]{2,1,0:T(8,128)S(1)}, u32[]{:S(2)}, u32[]{:S(2)}) %collective-permute-start.3) | collective-permute-done | bytes 131104 | tf_op jit(solution)/shard_map/ppermute | solution.py:279
  12.0 0.7 collective-permute-start.7
  12.7 0.7 collective-permute-start.6
  13.6 0.7 collective-permute-start.10
  14.3 1.3 %collective-permute-start.9 = (f32[10,128,128]{2,1,0:T(8,128)S(1)}, f32[10,128,128]{2,1,0:T(8,128)S(1)}, u32[]{:S(2)}, u32[]{:S(2)}) collective-permute-start(f32[10,128,128]{2,1,0:T(8,128)S(1)} %pad_maximum_fusion.1), channel_id=1, source_target_pairs={{0,2},{4,6},{32,34},{36,38},{64,66},{68,70},{96,98},{100,102},{9,1... | collective-permute-start | bytes 1966088 | tf_op jit(solution)/shard_map/ppermute | solution.py:279
  15.6 0.7 collective-permute-start.8
  16.3 4.4 %collective-permute-start.15 = (f32[128,8,128]{2,1,0:T(8,128)S(1)}, f32[128,8,128]{2,1,0:T(8,128)S(1)}, u32[]{:S(2)}, u32[]{:S(2)}) collective-permute-start(f32[128,8,128]{2,1,0:T(8,128)S(1)} %get-tuple-element.22), channel_id=1, source_target_pairs={{0,32},{1,33},{2,34},{3,35},{4,36},{5,37},{6,38},{7,39},{8,40},{9,... | collective-permute-start | bytes 1572872 | tf_op jit(solution)/shard_map/ppermute | solution.py:279
  20.8 1.3 %collective-permute-start.17 = (f32[128,8,128]{2,1,0:T(8,128)S(1)}, f32[128,8,128]{2,1,0:T(8,128)S(1)}, u32[]{:S(2)}, u32[]{:S(2)}) collective-permute-start(f32[128,8,128]{2,1,0:T(8,128)S(1)} %get-tuple-element.22), channel_id=1, source_target_pairs={{0,96},{1,97},{2,98},{3,99},{4,100},{5,101},{6,102},{7,103},{8,104... | collective-permute-start | bytes 1572872 | tf_op jit(solution)/shard_map/ppermute | solution.py:279
  22.1 9.1 %collective-permute-done.15 = f32[128,8,128]{2,1,0:T(8,128)S(1)} collective-permute-done((f32[128,8,128]{2,1,0:T(8,128)S(1)}, f32[128,8,128]{2,1,0:T(8,128)S(1)}, u32[]{:S(2)}, u32[]{:S(2)}) %collective-permute-start.15) | collective-permute-done | bytes 524320 | tf_op jit(solution)/shard_map/ppermute | solution.py:279
  31.2 0.7 collective-permute-start.16
  31.9 12.4 %collective-permute-done.9 = f32[10,128,128]{2,1,0:T(8,128)S(1)} collective-permute-done((f32[10,128,128]{2,1,0:T(8,128)S(1)}, f32[10,128,128]{2,1,0:T(8,128)S(1)}, u32[]{:S(2)}, u32[]{:S(2)}) %collective-permute-start.9) | collective-permute-done | bytes 655392 | tf_op jit(solution)/shard_map/ppermute | solution.py:279
  44.6 1.3 %collective-permute-done.11.other_ref = f32[2,128,128]{2,1,0:T(8,128)S(1)} collective-permute-done((f32[2,128,128]{2,1,0:T(8,128)S(1)}, f32[2,128,128]{2,1,0:T(8,128)S(1)}, u32[]{:S(2)}, u32[]{:S(2)}) %collective-permute-start.11) | collective-permute-done | bytes 131104 | tf_op jit(solution)/shard_map/ppermute | solution.py:279
  45.9 2.0 %collective-permute-start.12 = (f32[4,256,128]{2,1,0:T(8,128)S(1)}, f32[4,256,128]{2,1,0:T(8,128)S(1)}, u32[]{:S(2)}, u32[]{:S(2)}) collective-permute-start(f32[4,256,128]{2,1,0:T(8,128)S(1)} %bitcast.18), channel_id=1, source_target_pairs={{0,12},{1,13},{2,14},{3,15},{32,44},{33,45},{34,46},{35,47},{64,76... | collective-permute-start | bytes 1572872 | tf_op jit(solution)/shard_map/ppermute | solution.py:279
  48.2 8.6 %corner_factor.1 = (f32[256,256]{1,0:T(8,128)S(1)}, f32[256,256]{1,0:T(8,128)S(1)}, f32[256,256]{1,0:T(8,128)S(1)}) custom-call(s32[1]{0:T(128)} %bitcast.2.where_ref, f32[2,128,128]{2,1,0:T(8,128)S(1)} %slice.8.mine_ref, f32[2,128,128]{2,1,0:T(8,128)S(1)} %collective-permute-done.11.other_ref), custom_call_target="tpu_custom_call" | custom-call | flops 8000000000 | bytes 1000000 | tf_op jit(solution)/shard_map/corner_factor/pallas_call | solution.py:124
  56.9 3.8 %collective-permute-done.14.gp_ref = f32[4,256,128]{2,1,0:T(8,128)S(1)} collective-permute-done((f32[4,256,128]{2,1,0:T(8,128)S(1)}, f32[4,256,128]{2,1,0:T(8,128)S(1)}, u32[]{:S(2)}, u32[]{:S(2)}) %collective-permute-start.14) | collective-permute-done | bytes 524320 | tf_op jit(solution)/shard_map/ppermute | solution.py:279
  60.7 2.1 %collective-permute-done.12.gm_ref = f32[4,256,128]{2,1,0:T(8,128)S(1)} collective-permute-done((f32[4,256,128]{2,1,0:T(8,128)S(1)}, f32[4,256,128]{2,1,0:T(8,128)S(1)}, u32[]{:S(2)}, u32[]{:S(2)}) %collective-permute-start.12) | collective-permute-done | bytes 524320 | tf_op jit(solution)/shard_map/ppermute | solution.py:279
  62.8 9.0 %trailing_update.1 = f32[2048,8,128]{2,1,0:T(8,128)} custom-call(s32[6]{0:T(128)S(1)} %stack.50.place_ref, f32[256,256]{1,0:T(8,128)S(1)} %get-tuple-element.17.lower_ref, f32[256,256]{1,0:T(8,128)S(1)} %get-tuple-element.18.inverse_ref, f32[256,256]{1,0:T(8,128)S(1)} %get-tuple-element.19.whole_ref, f32[4,256,128]{2,1,0:T(8,128)S(1)} %bitcast.19, ...), custom_call_target="tpu_custom_call" | custom-call | flops 4000000000 | bytes 20000000 | tf_op jit(solution)/shard_map/trailing_update/pallas_call | solution.py:229
  (29 shorter events, 1.0 us)
Async XLA Ops:
  1.8 0.7 collective-permute-start.2
  2.5 7.9 %collective-permute-start.4 = (f32[2,128,128]{2,1,0:T(8,128)S(1)}, f32[2,128,128]{2,1,0:T(8,128)S(1)}, u32[]{:S(2)}, u32[]{:S(2)}) collective-permute-start(f32[2,128,128]{2,1,0:T(8,128)S(1)} %fusion), channel_id=1, source_target_pairs={{0,64},{1,65},{2,66},{3,67},{4,68},{5,69},{6,70},{7,71},{8,72},{9,... | collective-permute-start | bytes 393224 | tf_op jit(solution)/shard_map/ppermute | solution.py:279
  6.4 4.0 %collective-permute-start.5 = (f32[2,128,128]{2,1,0:T(8,128)S(1)}, f32[2,128,128]{2,1,0:T(8,128)S(1)}, u32[]{:S(2)}, u32[]{:S(2)}) collective-permute-start(f32[2,128,128]{2,1,0:T(8,128)S(1)} %fusion), channel_id=1, source_target_pairs={{0,96},{1,97},{2,98},{3,99},{4,100},{5,101},{6,102},{7,103},{8,104... | collective-permute-start | bytes 393224 | tf_op jit(solution)/shard_map/ppermute | solution.py:279
  7.7 4.2 %collective-permute-start.3 = (f32[2,128,128]{2,1,0:T(8,128)S(1)}, f32[2,128,128]{2,1,0:T(8,128)S(1)}, u32[]{:S(2)}, u32[]{:S(2)}) collective-permute-start(f32[2,128,128]{2,1,0:T(8,128)S(1)} %fusion), channel_id=1, source_target_pairs={{0,32},{1,33},{2,34},{3,35},{4,36},{5,37},{6,38},{7,39},{8,40},{9,... | collective-permute-start | bytes 393224 | tf_op jit(solution)/shard_map/ppermute | solution.py:279
  9.0 4.4 %collective-permute-start = (f32[4,256,128]{2,1,0:T(8,128)S(1)}, f32[4,256,128]{2,1,0:T(8,128)S(1)}, u32[]{:S(2)}, u32[]{:S(2)}) collective-permute-start(f32[4,256,128]{2,1,0:T(8,128)S(1)} %get-tuple-element.15), channel_id=1, source_target_pairs={{0,4},{32,36},{64,68},{96,100},{1,13},{33,45},{65,77},{97,109},{16... | collective-permute-start | bytes 1572872 | tf_op jit(solution)/shard_map/ppermute | solution.py:279
  9.7 3.7 %collective-permute-start.1 = (f32[4,256,128]{2,1,0:T(8,128)S(1)}, f32[4,256,128]{2,1,0:T(8,128)S(1)}, u32[]{:S(2)}, u32[]{:S(2)}) collective-permute-start(f32[4,256,128]{2,1,0:T(8,128)S(1)} %get-tuple-element.14), channel_id=1, source_target_pairs={{1,9},{33,41},{65,73},{97,105}} | collective-permute-start | bytes 1572872 | tf_op jit(solution)/shard_map/ppermute | solution.py:279
  12.0 1.4 %collective-permute-start.7 = (f32[2,128,128]{2,1,0:T(8,128)S(1)}, f32[2,128,128]{2,1,0:T(8,128)S(1)}, u32[]{:S(2)}, u32[]{:S(2)}) collective-permute-start(f32[2,128,128]{2,1,0:T(8,128)S(1)} %add_add_fusion.1), channel_id=1, source_target_pairs={{1,9},{33,41},{65,73},{97,105}} | collective-permute-start | bytes 393224 | tf_op jit(solution)/shard_map/ppermute | solution.py:279
  12.7 0.7 collective-permute-start.6
  13.6 18.3 %collective-permute-start.10 = (f32[10,128,128]{2,1,0:T(8,128)S(1)}, f32[10,128,128]{2,1,0:T(8,128)S(1)}, u32[]{:S(2)}, u32[]{:S(2)}) collective-permute-start(f32[10,128,128]{2,1,0:T(8,128)S(1)} %pad_maximum_fusion.1), channel_id=1, source_target_pairs={{0,3},{4,7},{32,35},{36,39},{64,67},{68,71},{96,99},{100,103},{9,8... | collective-permute-start | bytes 1966088 | tf_op jit(solution)/shard_map/ppermute | solution.py:279
  14.3 29.9 %collective-permute-start.9 = (f32[10,128,128]{2,1,0:T(8,128)S(1)}, f32[10,128,128]{2,1,0:T(8,128)S(1)}, u32[]{:S(2)}, u32[]{:S(2)}) collective-permute-start(f32[10,128,128]{2,1,0:T(8,128)S(1)} %pad_maximum_fusion.1), channel_id=1, source_target_pairs={{0,2},{4,6},{32,34},{36,38},{64,66},{68,70},{96,98},{100,102},{9,1... | collective-permute-start | bytes 1966088 | tf_op jit(solution)/shard_map/ppermute | solution.py:279
  15.6 28.6 %collective-permute-start.8 = (f32[10,128,128]{2,1,0:T(8,128)S(1)}, f32[10,128,128]{2,1,0:T(8,128)S(1)}, u32[]{:S(2)}, u32[]{:S(2)}) collective-permute-start(f32[10,128,128]{2,1,0:T(8,128)S(1)} %pad_maximum_fusion.1), channel_id=1, source_target_pairs={{0,1},{4,5},{32,33},{36,37},{64,65},{68,69},{96,97},{100,101},{9,1... | collective-permute-start | bytes 1966088 | tf_op jit(solution)/shard_map/ppermute | solution.py:279
  16.3 14.9 %collective-permute-start.15 = (f32[128,8,128]{2,1,0:T(8,128)S(1)}, f32[128,8,128]{2,1,0:T(8,128)S(1)}, u32[]{:S(2)}, u32[]{:S(2)}) collective-permute-start(f32[128,8,128]{2,1,0:T(8,128)S(1)} %get-tuple-element.22), channel_id=1, source_target_pairs={{0,32},{1,33},{2,34},{3,35},{4,36},{5,37},{6,38},{7,39},{8,40},{9,... | collective-permute-start | bytes 1572872 | tf_op jit(solution)/shard_map/ppermute | solution.py:279
  20.8 27.1 %collective-permute-start.17 = (f32[128,8,128]{2,1,0:T(8,128)S(1)}, f32[128,8,128]{2,1,0:T(8,128)S(1)}, u32[]{:S(2)}, u32[]{:S(2)}) collective-permute-start(f32[128,8,128]{2,1,0:T(8,128)S(1)} %get-tuple-element.22), channel_id=1, source_target_pairs={{0,96},{1,97},{2,98},{3,99},{4,100},{5,101},{6,102},{7,103},{8,104... | collective-permute-start | bytes 1572872 | tf_op jit(solution)/shard_map/ppermute | solution.py:279
  31.2 16.7 %collective-permute-start.16 = (f32[128,8,128]{2,1,0:T(8,128)S(1)}, f32[128,8,128]{2,1,0:T(8,128)S(1)}, u32[]{:S(2)}, u32[]{:S(2)}) collective-permute-start(f32[128,8,128]{2,1,0:T(8,128)S(1)} %collective-permute-done.15), channel_id=1, source_target_pairs={{32,64},{33,65},{34,66},{35,67},{36,68},{37,69},{38,70},{39,71},{4... | collective-permute-start | bytes 1572872 | tf_op jit(solution)/shard_map/ppermute | solution.py:279
  44.4 1.4 %collective-permute-start.11 = (f32[2,128,128]{2,1,0:T(8,128)S(1)}, f32[2,128,128]{2,1,0:T(8,128)S(1)}, u32[]{:S(2)}, u32[]{:S(2)}) collective-permute-start(f32[2,128,128]{2,1,0:T(8,128)S(1)} %slice.8.mine_ref), channel_id=1, source_target_pairs={{0,16},{1,17},{2,18},{3,19},{4,20},{5,21},{6,22},{7,23},{8,24},{9,... | collective-permute-start | bytes 393224 | tf_op jit(solution)/shard_map/ppermute | solution.py:279
  45.8 14.8 %collective-permute-start.14 = (f32[4,256,128]{2,1,0:T(8,128)S(1)}, f32[4,256,128]{2,1,0:T(8,128)S(1)}, u32[]{:S(2)}, u32[]{:S(2)}) collective-permute-start(f32[4,256,128]{2,1,0:T(8,128)S(1)} %bitcast.16), channel_id=1, source_target_pairs={{0,4},{1,5},{2,6},{3,7},{32,36},{33,37},{34,38},{35,39},{64,68},{6... | collective-permute-start | bytes 1572872 | tf_op jit(solution)/shard_map/ppermute | solution.py:279
  45.9 14.8 %collective-permute-start.13 = (f32[4,256,128]{2,1,0:T(8,128)S(1)}, f32[4,256,128]{2,1,0:T(8,128)S(1)}, u32[]{:S(2)}, u32[]{:S(2)}) collective-permute-start(f32[4,256,128]{2,1,0:T(8,128)S(1)} %bitcast.17), channel_id=1, source_target_pairs={{0,8},{1,9},{2,10},{3,11},{32,40},{33,41},{34,42},{35,43},{64,72},... | collective-permute-start | bytes 1572872 | tf_op jit(solution)/shard_map/ppermute | solution.py:279
  45.9 16.9 %collective-permute-start.12 = (f32[4,256,128]{2,1,0:T(8,128)S(1)}, f32[4,256,128]{2,1,0:T(8,128)S(1)}, u32[]{:S(2)}, u32[]{:S(2)}) collective-permute-start(f32[4,256,128]{2,1,0:T(8,128)S(1)} %bitcast.18), channel_id=1, source_target_pairs={{0,12},{1,13},{2,14},{3,15},{32,44},{33,45},{34,46},{35,47},{64,76... | collective-permute-start | bytes 1572872 | tf_op jit(solution)/shard_map/ppermute | solution.py:279
  48.1 8.7 %collective-permute-start.18 = (f32[128,8,128]{2,1,0:T(8,128)S(1)}, f32[128,8,128]{2,1,0:T(8,128)S(1)}, u32[]{:S(2)}, u32[]{:S(2)}) collective-permute-start(f32[128,8,128]{2,1,0:T(8,128)S(1)} %add_select_fusion), channel_id=1, source_target_pairs={{0,16},{1,17},{2,18},{3,19},{4,20},{5,21},{6,22},{7,23},{8,24},{9,... | collective-permute-start | bytes 1572872 | tf_op jit(solution)/shard_map/ppermute | solution.py:279

commit v5 on v4

--- a/solution.py
+++ b/solution.py
@@ -372,8 +372,8 @@
     ]
     b1, b3, b2 = (send(own, moves) for moves in lines)
     top = after(top, own)
-    c1, c3 = (send(top, along_x([(0, to)])) for to in (1, 3))
-    c2 = send(c1, along_x([(1, 2)]))
+    c = jnp.where(x == 0, top, send(top, along_x([(0, 1)])))
+    c2 = send(c, along_x([(0, 3), (1, 2)]))
     g = own + b1 + b2 + b3
     e, g = g[8:], g[:8].reshape(4, TR, NB)
 
@@ -387,7 +387,7 @@
         for d in (1, 3, 2)
     ]
     g1, g3, g2 = (send(g, moves) for moves in around)
-    c = jnp.where(x == 0, top, c1 + c2 + c3)
+    c = jnp.where(x < 2, c, c2)
     lower, inverse, whole = factor_corner(place[2:3], mine, other)
     columns = jnp.stack([c, send(c, SWAP)])
     columns = jnp.where(core == 0, columns, columns[::-1])

time: 72.3 us -> 74.3 us (1.028)
  the two profiles are of different devices: /device:TPU:88 before, /device:TPU:24 now
where the time goes in v5:
time: 74.3 us; the launch traced here: 74 us
  starting transfers between devices  35.6 us (48%)
  Pallas kernels  19.4 us (26%)
  waiting for transfers between devices  17.8 us (24%)
    ppermute x18, starting transfers between devices, send(): return lax.ppermute(value, BOTH, moves)  35.6 us
    ppermute x18, waiting for transfers between devices, send(): return lax.ppermute(value, BOTH, moves)  17.8 us
    pallas_call x1, Pallas kernels, update_trailing(): pl.pallas_call(trailing_kernel, out_shape=jax.ShapeDtypeStruct(m.shape, F...  9.18 us
    pallas_call x1, Pallas kernels, factor_corner(): pl.pallas_call(factor_kernel, out_shape=(jax.ShapeDtypeStruct((W2, W2), F...  8.57 us
    pallas_call x1, Pallas kernels, extract(): pl.pallas_call(extract_kernel, out_shape=(half, half, jax.ShapeDtypeStruc...  1.68 us
  transfers between devices with their start and end apart: 18, of which 5 were waited for; matrix products, arithmetic and copies ran while one was open for 1% of the time, Pallas kernels for 12%

profile of v5, /device:TPU:24, one launch (start us, length us, event | category | flops | bytes accessed | tf_op | source)
XLA Modules:
  0.0 74.0 jit_solution(1847836075039705828)
XLA Ops:
  0.1 1.7 %extract_panels.1 = (f32[4,256,128]{2,1,0:T(8,128)S(1)}, f32[4,256,128]{2,1,0:T(8,128)S(1)}, f32[128,128]{1,0:T(8,128)S(1)}, f32[128,8,128]{2,1,0:T(8,128)S(1)}) custom-call(s32[6]{0:T(128)S(1)} %stack.50.place_ref, f32[2048,8,128]{2,1,0:T(8,128)} %bitcast.22), custom_call_target="tpu_custom_call" | custom-call | bytes 4000000 | tf_op jit(solution)/shard_map/extract_panels/pallas_call | solution.py:328
  1.8 0.7 collective-permute-start.2
  2.5 3.9 %collective-permute-start.4 = (f32[2,128,128]{2,1,0:T(8,128)S(1)}, f32[2,128,128]{2,1,0:T(8,128)S(1)}, u32[]{:S(2)}, u32[]{:S(2)}) collective-permute-start(f32[2,128,128]{2,1,0:T(8,128)S(1)} %fusion), channel_id=1, source_target_pairs={{0,64},{1,65},{2,66},{3,67},{4,68},{5,69},{6,70},{7,71},{8,72},{9,... | collective-permute-start | bytes 393224 | tf_op jit(solution)/shard_map/ppermute | solution.py:279
  6.4 1.3 %collective-permute-start.5 = (f32[2,128,128]{2,1,0:T(8,128)S(1)}, f32[2,128,128]{2,1,0:T(8,128)S(1)}, u32[]{:S(2)}, u32[]{:S(2)}) collective-permute-start(f32[2,128,128]{2,1,0:T(8,128)S(1)} %fusion), channel_id=1, source_target_pairs={{0,96},{1,97},{2,98},{3,99},{4,100},{5,101},{6,102},{7,103},{8,104... | collective-permute-start | bytes 393224 | tf_op jit(solution)/shard_map/ppermute | solution.py:279
  7.7 1.3 %collective-permute-start.3 = (f32[2,128,128]{2,1,0:T(8,128)S(1)}, f32[2,128,128]{2,1,0:T(8,128)S(1)}, u32[]{:S(2)}, u32[]{:S(2)}) collective-permute-start(f32[2,128,128]{2,1,0:T(8,128)S(1)} %fusion), channel_id=1, source_target_pairs={{0,32},{1,33},{2,34},{3,35},{4,36},{5,37},{6,38},{7,39},{8,40},{9,... | collective-permute-start | bytes 393224 | tf_op jit(solution)/shard_map/ppermute | solution.py:279
  9.0 0.7 collective-permute-start
  9.7 0.7 collective-permute-start.1
  10.5 1.5 %collective-permute-done.3 = f32[2,128,128]{2,1,0:T(8,128)S(1)} collective-permute-done((f32[2,128,128]{2,1,0:T(8,128)S(1)}, f32[2,128,128]{2,1,0:T(8,128)S(1)}, u32[]{:S(2)}, u32[]{:S(2)}) %collective-permute-start.3) | collective-permute-done | bytes 131104 | tf_op jit(solution)/shard_map/ppermute | solution.py:279
  12.0 0.7 collective-permute-start.7
  12.7 0.7 collective-permute-start.6
  13.6 4.4 %collective-permute-start.15 = (f32[128,8,128]{2,1,0:T(8,128)S(1)}, f32[128,8,128]{2,1,0:T(8,128)S(1)}, u32[]{:S(2)}, u32[]{:S(2)}) collective-permute-start(f32[128,8,128]{2,1,0:T(8,128)S(1)} %get-tuple-element.22), channel_id=1, source_target_pairs={{0,32},{1,33},{2,34},{3,35},{4,36},{5,37},{6,38},{7,39},{8,40},{9,... | collective-permute-start | bytes 1572872 | tf_op jit(solution)/shard_map/ppermute | solution.py:279
  18.0 1.3 %collective-permute-start.10 = (f32[10,128,128]{2,1,0:T(8,128)S(1)}, f32[10,128,128]{2,1,0:T(8,128)S(1)}, u32[]{:S(2)}, u32[]{:S(2)}) collective-permute-start(f32[10,128,128]{2,1,0:T(8,128)S(1)} %pad_maximum_fusion.1), channel_id=1, source_target_pairs={{0,3},{4,7},{32,35},{36,39},{64,67},{68,71},{96,99},{100,103},{9,8... | collective-permute-start | bytes 1966088 | tf_op jit(solution)/shard_map/ppermute | solution.py:279
  19.3 0.7 collective-permute-start.9
  20.0 0.7 collective-permute-start.8
  20.8 5.1 %collective-permute-done.15 = f32[128,8,128]{2,1,0:T(8,128)S(1)} collective-permute-done((f32[128,8,128]{2,1,0:T(8,128)S(1)}, f32[128,8,128]{2,1,0:T(8,128)S(1)}, u32[]{:S(2)}, u32[]{:S(2)}) %collective-permute-start.15) | collective-permute-done | bytes 524320 | tf_op jit(solution)/shard_map/ppermute | solution.py:279
  25.9 1.3 %collective-permute-start.16 = (f32[128,8,128]{2,1,0:T(8,128)S(1)}, f32[128,8,128]{2,1,0:T(8,128)S(1)}, u32[]{:S(2)}, u32[]{:S(2)}) collective-permute-start(f32[128,8,128]{2,1,0:T(8,128)S(1)} %broadcast_select_fusion), channel_id=1, source_target_pairs={{0,96},{1,97},{2,98},{3,99},{4,100},{5,101},{6,102},{7,103},{8,104... | collective-permute-start | bytes 1572872 | tf_op jit(solution)/shard_map/ppermute | solution.py:279
  27.2 6.7 %collective-permute-done.10 = f32[10,128,128]{2,1,0:T(8,128)S(1)} collective-permute-done((f32[10,128,128]{2,1,0:T(8,128)S(1)}, f32[10,128,128]{2,1,0:T(8,128)S(1)}, u32[]{:S(2)}, u32[]{:S(2)}) %collective-permute-start.10) | collective-permute-done | bytes 655392 | tf_op jit(solution)/shard_map/ppermute | solution.py:279
  34.1 6.4 %collective-permute-start.11 = (f32[2,128,128]{2,1,0:T(8,128)S(1)}, f32[2,128,128]{2,1,0:T(8,128)S(1)}, u32[]{:S(2)}, u32[]{:S(2)}) collective-permute-start(f32[2,128,128]{2,1,0:T(8,128)S(1)} %slice.8.mine_ref), channel_id=1, source_target_pairs={{0,16},{1,17},{2,18},{3,19},{4,20},{5,21},{6,22},{7,23},{8,24},{9,... | collective-permute-start | bytes 393224 | tf_op jit(solution)/shard_map/ppermute | solution.py:279
  40.6 0.9 %collective-permute-done.11.other_ref = f32[2,128,128]{2,1,0:T(8,128)S(1)} collective-permute-done((f32[2,128,128]{2,1,0:T(8,128)S(1)}, f32[2,128,128]{2,1,0:T(8,128)S(1)}, u32[]{:S(2)}, u32[]{:S(2)}) %collective-permute-start.11) | collective-permute-done | bytes 131104 | tf_op jit(solution)/shard_map/ppermute | solution.py:279
  41.5 2.2 %collective-permute-start.14 = (f32[4,256,128]{2,1,0:T(8,128)S(1)}, f32[4,256,128]{2,1,0:T(8,128)S(1)}, u32[]{:S(2)}, u32[]{:S(2)}) collective-permute-start(f32[4,256,128]{2,1,0:T(8,128)S(1)} %bitcast.16), channel_id=1, source_target_pairs={{0,4},{1,5},{2,6},{3,7},{32,36},{33,37},{34,38},{35,39},{64,68},{6... | collective-permute-start | bytes 1572872 | tf_op jit(solution)/shard_map/ppermute | solution.py:279
  43.7 8.2 %collective-permute-start.13 = (f32[4,256,128]{2,1,0:T(8,128)S(1)}, f32[4,256,128]{2,1,0:T(8,128)S(1)}, u32[]{:S(2)}, u32[]{:S(2)}) collective-permute-start(f32[4,256,128]{2,1,0:T(8,128)S(1)} %bitcast.17), channel_id=1, source_target_pairs={{0,8},{1,9},{2,10},{3,11},{32,40},{33,41},{34,42},{35,43},{64,72},... | collective-permute-start | bytes 1572872 | tf_op jit(solution)/shard_map/ppermute | solution.py:279
  52.4 8.6 %corner_factor.1 = (f32[256,256]{1,0:T(8,128)S(1)}, f32[256,256]{1,0:T(8,128)S(1)}, f32[256,256]{1,0:T(8,128)S(1)}) custom-call(s32[1]{0:T(128)} %bitcast.2.where_ref, f32[2,128,128]{2,1,0:T(8,128)S(1)} %slice.8.mine_ref, f32[2,128,128]{2,1,0:T(8,128)S(1)} %collective-permute-done.11.other_ref), custom_call_target="tpu_custom_call" | custom-call | flops 8000000000 | bytes 1000000 | tf_op jit(solution)/shard_map/corner_factor/pallas_call | solution.py:124
  61.1 3.5 %collective-permute-done.13.gf_ref = f32[4,256,128]{2,1,0:T(8,128)S(1)} collective-permute-done((f32[4,256,128]{2,1,0:T(8,128)S(1)}, f32[4,256,128]{2,1,0:T(8,128)S(1)}, u32[]{:S(2)}, u32[]{:S(2)}) %collective-permute-start.13) | collective-permute-done | bytes 524320 | tf_op jit(solution)/shard_map/ppermute | solution.py:279
  64.6 9.2 %trailing_update.1 = f32[2048,8,128]{2,1,0:T(8,128)} custom-call(s32[6]{0:T(128)S(1)} %stack.50.place_ref, f32[256,256]{1,0:T(8,128)S(1)} %get-tuple-element.17.lower_ref, f32[256,256]{1,0:T(8,128)S(1)} %get-tuple-element.18.inverse_ref, f32[256,256]{1,0:T(8,128)S(1)} %get-tuple-element.19.whole_ref, f32[4,256,128]{2,1,0:T(8,128)S(1)} %bitcast.19, ...), custom_call_target="tpu_custom_call" | custom-call | flops 4000000000 | bytes 20000000 | tf_op jit(solution)/shard_map/trailing_update/pallas_call | solution.py:229
  (28 shorter events, 1.3 us)
Async XLA Ops:
  1.8 0.7 collective-permute-start.2
  2.5 7.9 %collective-permute-start.4 = (f32[2,128,128]{2,1,0:T(8,128)S(1)}, f32[2,128,128]{2,1,0:T(8,128)S(1)}, u32[]{:S(2)}, u32[]{:S(2)}) collective-permute-start(f32[2,128,128]{2,1,0:T(8,128)S(1)} %fusion), channel_id=1, source_target_pairs={{0,64},{1,65},{2,66},{3,67},{4,68},{5,69},{6,70},{7,71},{8,72},{9,... | collective-permute-start | bytes 393224 | tf_op jit(solution)/shard_map/ppermute | solution.py:279
  6.4 4.0 %collective-permute-start.5 = (f32[2,128,128]{2,1,0:T(8,128)S(1)}, f32[2,128,128]{2,1,0:T(8,128)S(1)}, u32[]{:S(2)}, u32[]{:S(2)}) collective-permute-start(f32[2,128,128]{2,1,0:T(8,128)S(1)} %fusion), channel_id=1, source_target_pairs={{0,96},{1,97},{2,98},{3,99},{4,100},{5,101},{6,102},{7,103},{8,104... | collective-permute-start | bytes 393224 | tf_op jit(solution)/shard_map/ppermute | solution.py:279
  7.7 4.2 %collective-permute-start.3 = (f32[2,128,128]{2,1,0:T(8,128)S(1)}, f32[2,128,128]{2,1,0:T(8,128)S(1)}, u32[]{:S(2)}, u32[]{:S(2)}) collective-permute-start(f32[2,128,128]{2,1,0:T(8,128)S(1)} %fusion), channel_id=1, source_target_pairs={{0,32},{1,33},{2,34},{3,35},{4,36},{5,37},{6,38},{7,39},{8,40},{9,... | collective-permute-start | bytes 393224 | tf_op jit(solution)/shard_map/ppermute | solution.py:279
  9.0 4.4 %collective-permute-start = (f32[4,256,128]{2,1,0:T(8,128)S(1)}, f32[4,256,128]{2,1,0:T(8,128)S(1)}, u32[]{:S(2)}, u32[]{:S(2)}) collective-permute-start(f32[4,256,128]{2,1,0:T(8,128)S(1)} %get-tuple-element.15), channel_id=1, source_target_pairs={{0,4},{32,36},{64,68},{96,100},{1,13},{33,45},{65,77},{97,109},{16... | collective-permute-start | bytes 1572872 | tf_op jit(solution)/shard_map/ppermute | solution.py:279
  9.7 3.7 %collective-permute-start.1 = (f32[4,256,128]{2,1,0:T(8,128)S(1)}, f32[4,256,128]{2,1,0:T(8,128)S(1)}, u32[]{:S(2)}, u32[]{:S(2)}) collective-permute-start(f32[4,256,128]{2,1,0:T(8,128)S(1)} %get-tuple-element.14), channel_id=1, source_target_pairs={{1,9},{33,41},{65,73},{97,105}} | collective-permute-start | bytes 1572872 | tf_op jit(solution)/shard_map/ppermute | solution.py:279
  12.0 1.4 %collective-permute-start.7 = (f32[2,128,128]{2,1,0:T(8,128)S(1)}, f32[2,128,128]{2,1,0:T(8,128)S(1)}, u32[]{:S(2)}, u32[]{:S(2)}) collective-permute-start(f32[2,128,128]{2,1,0:T(8,128)S(1)} %add_add_fusion.1), channel_id=1, source_target_pairs={{1,9},{33,41},{65,73},{97,105}} | collective-permute-start | bytes 393224 | tf_op jit(solution)/shard_map/ppermute | solution.py:279
  12.7 0.7 collective-permute-start.6
  13.6 12.2 %collective-permute-start.15 = (f32[128,8,128]{2,1,0:T(8,128)S(1)}, f32[128,8,128]{2,1,0:T(8,128)S(1)}, u32[]{:S(2)}, u32[]{:S(2)}) collective-permute-start(f32[128,8,128]{2,1,0:T(8,128)S(1)} %get-tuple-element.22), channel_id=1, source_target_pairs={{0,32},{1,33},{2,34},{3,35},{4,36},{5,37},{6,38},{7,39},{8,40},{9,... | collective-permute-start | bytes 1572872 | tf_op jit(solution)/shard_map/ppermute | solution.py:279
  18.0 15.9 %collective-permute-start.10 = (f32[10,128,128]{2,1,0:T(8,128)S(1)}, f32[10,128,128]{2,1,0:T(8,128)S(1)}, u32[]{:S(2)}, u32[]{:S(2)}) collective-permute-start(f32[10,128,128]{2,1,0:T(8,128)S(1)} %pad_maximum_fusion.1), channel_id=1, source_target_pairs={{0,3},{4,7},{32,35},{36,39},{64,67},{68,71},{96,99},{100,103},{9,8... | collective-permute-start | bytes 1966088 | tf_op jit(solution)/shard_map/ppermute | solution.py:279
  19.3 14.6 %collective-permute-start.9 = (f32[10,128,128]{2,1,0:T(8,128)S(1)}, f32[10,128,128]{2,1,0:T(8,128)S(1)}, u32[]{:S(2)}, u32[]{:S(2)}) collective-permute-start(f32[10,128,128]{2,1,0:T(8,128)S(1)} %pad_maximum_fusion.1), channel_id=1, source_target_pairs={{0,2},{4,6},{32,34},{36,38},{64,66},{68,70},{96,98},{100,102},{9,1... | collective-permute-start | bytes 1966088 | tf_op jit(solution)/shard_map/ppermute | solution.py:279
  20.0 13.9 %collective-permute-start.8 = (f32[10,128,128]{2,1,0:T(8,128)S(1)}, f32[10,128,128]{2,1,0:T(8,128)S(1)}, u32[]{:S(2)}, u32[]{:S(2)}) collective-permute-start(f32[10,128,128]{2,1,0:T(8,128)S(1)} %pad_maximum_fusion.1), channel_id=1, source_target_pairs={{0,1},{4,5},{32,33},{36,37},{64,65},{68,69},{96,97},{100,101},{9,1... | collective-permute-start | bytes 1966088 | tf_op jit(solution)/shard_map/ppermute | solution.py:279
  25.9 26.3 %collective-permute-start.16 = (f32[128,8,128]{2,1,0:T(8,128)S(1)}, f32[128,8,128]{2,1,0:T(8,128)S(1)}, u32[]{:S(2)}, u32[]{:S(2)}) collective-permute-start(f32[128,8,128]{2,1,0:T(8,128)S(1)} %broadcast_select_fusion), channel_id=1, source_target_pairs={{0,96},{1,97},{2,98},{3,99},{4,100},{5,101},{6,102},{7,103},{8,104... | collective-permute-start | bytes 1572872 | tf_op jit(solution)/shard_map/ppermute | solution.py:279
  34.1 7.4 %collective-permute-start.11 = (f32[2,128,128]{2,1,0:T(8,128)S(1)}, f32[2,128,128]{2,1,0:T(8,128)S(1)}, u32[]{:S(2)}, u32[]{:S(2)}) collective-permute-start(f32[2,128,128]{2,1,0:T(8,128)S(1)} %slice.8.mine_ref), channel_id=1, source_target_pairs={{0,16},{1,17},{2,18},{3,19},{4,20},{5,21},{6,22},{7,23},{8,24},{9,... | collective-permute-start | bytes 393224 | tf_op jit(solution)/shard_map/ppermute | solution.py:279
  41.5 19.6 %collective-permute-start.14 = (f32[4,256,128]{2,1,0:T(8,128)S(1)}, f32[4,256,128]{2,1,0:T(8,128)S(1)}, u32[]{:S(2)}, u32[]{:S(2)}) collective-permute-start(f32[4,256,128]{2,1,0:T(8,128)S(1)} %bitcast.16), channel_id=1, source_target_pairs={{0,4},{1,5},{2,6},{3,7},{32,36},{33,37},{34,38},{35,39},{64,68},{6... | collective-permute-start | bytes 1572872 | tf_op jit(solution)/shard_map/ppermute | solution.py:279
  43.7 20.9 %collective-permute-start.13 = (f32[4,256,128]{2,1,0:T(8,128)S(1)}, f32[4,256,128]{2,1,0:T(8,128)S(1)}, u32[]{:S(2)}, u32[]{:S(2)}) collective-permute-start(f32[4,256,128]{2,1,0:T(8,128)S(1)} %bitcast.17), channel_id=1, source_target_pairs={{0,8},{1,9},{2,10},{3,11},{32,40},{33,41},{34,42},{35,43},{64,72},... | collective-permute-start | bytes 1572872 | tf_op jit(solution)/shard_map/ppermute | solution.py:279
  51.8 12.8 %collective-permute-start.12 = (f32[4,256,128]{2,1,0:T(8,128)S(1)}, f32[4,256,128]{2,1,0:T(8,128)S(1)}, u32[]{:S(2)}, u32[]{:S(2)}) collective-permute-start(f32[4,256,128]{2,1,0:T(8,128)S(1)} %bitcast.18), channel_id=1, source_target_pairs={{0,12},{1,13},{2,14},{3,15},{32,44},{33,45},{34,46},{35,47},{64,76... | collective-permute-start | bytes 1572872 | tf_op jit(solution)/shard_map/ppermute | solution.py:279
  52.3 8.7 %collective-permute-start.17 = (f32[128,8,128]{2,1,0:T(8,128)S(1)}, f32[128,8,128]{2,1,0:T(8,128)S(1)}, u32[]{:S(2)}, u32[]{:S(2)}) collective-permute-start(f32[128,8,128]{2,1,0:T(8,128)S(1)} %broadcast_select_fusion.1), channel_id=1, source_target_pairs={{0,16},{1,17},{2,18},{3,19},{4,20},{5,21},{6,22},{7,23},{8,24},{9,... | collective-permute-start | bytes 1572872 | tf_op jit(solution)/shard_map/ppermute | solution.py:279
